TPU v7x, 512 devices: a whole 4x8x8 slice. The times are simulated.
512 devices in a mesh: phase: 8 (over z), ctx: 64 (over x, y, core).
Axes of the slice: x: 4, y: 8, z: 8, core: 2. Of those that a mesh axis runs over, the one named last changes fastest.
Arguments:
- activations: bfloat16 [8, 8192, 4096], P('phase', 'ctx'), may hold values from -6 to 6
- norm_gain: bfloat16 [8, 4096], P('phase'), may hold values from 0.25 to 1.75
- short_taps: bfloat16 [8, 3, 3, 4096], P('phase'), may hold values from -3 to 3
- skip_gain: bfloat16 [8, 4096], P('phase'), may hold values from 0.19921875 to 1.5
- time_const: float32 [8, 4096, 16], P('phase', 'ctx'), may hold values from 25 to 32768
- residues: float32 [8, 4096, 16], P('phase', 'ctx'), may hold values from -2 to 2
Outputs:
- handed: bfloat16 [8, 8192, 4096], P('phase', 'ctx')
All inputs are finite; a program needn't handle non-finite values.
Results may differ from a plain program's by a relative error of at most 0.0058.
Values may be sent and summed in bfloat16 or wider, within the bound.
A program may use at most 128 MiB of HBM per device.

v0:
```python
import math

import jax
import jax.numpy as jnp
from jax import lax
from jax.sharding import PartitionSpec as P

HIGHEST_PRECISION = lax.Precision.HIGHEST


def from_behind(shard, axis, by):
    count = lax.axis_size(axis)
    pairs = [(i, i + by) for i in range(count) if 0 <= i + by < count]
    return lax.ppermute(shard, axis, pairs)


def from_behind_2(block, axis, distance):
    devices = range(lax.axis_size(axis))
    route = [((i - distance) % len(devices), i) for i in devices]
    return lax.ppermute(block, axis, route)


def circle_angle(product, modulus):
    return 2.0 * math.pi / modulus * (product % modulus).astype(jnp.float32)


def filter_spectrum(decay_time, residue, frequency, padded_length, length):
    theta = circle_angle(frequency, padded_length)
    half_sine = jnp.sin(0.5 * theta)[None]
    full_sine = jnp.sin(theta)[None]
    parity = (1 - 2 * (frequency % 2)).astype(jnp.float32)[None]
    shape = (decay_time.shape[0],) + frequency.shape
    real_part = jnp.zeros(shape, jnp.float32)
    imag_part = jnp.zeros(shape, jnp.float32)
    for mode in range(decay_time.shape[1]):
        decay_rate = 1.0 / decay_time[:, mode][:, None, None]
        damping = jnp.exp(-decay_rate)
        leftover = -jnp.expm1(-decay_rate)
        weight = residue[:, mode][:, None, None] * jnp.sqrt(-jnp.expm1(-2.0 * decay_rate))
        numerator = weight * (1.0 - jnp.exp(-decay_rate * length) * parity)
        denom_real = leftover + 2.0 * damping * half_sine * half_sine
        denom_imag = damping * full_sine
        magnitude = denom_real * denom_real + denom_imag * denom_imag
        real_part = real_part + numerator * denom_real / magnitude
        imag_part = imag_part - numerator * denom_imag / magnitude
    return (real_part, imag_part)


def spectral_conv(mixed_in, decay_time, residue):
    devices = lax.axis_size("ctx")
    length, channels = mixed_in.shape
    local_channels = channels // devices
    sequence = length * devices
    pieces = jnp.transpose(mixed_in).reshape(devices, local_channels, length)
    lines = lax.all_to_all(pieces, "ctx", split_axis=0, concat_axis=2, tiled=True)[0]
    col_count = 128
    padded_length = 2 * sequence
    row_count = padded_length // col_count
    used_rows = row_count // 2
    row_index = jnp.arange(row_count, dtype=jnp.int32)
    used_index = jnp.arange(used_rows, dtype=jnp.int32)
    col_index = jnp.arange(col_count, dtype=jnp.int32)
    row_angle = circle_angle(row_index[:, None] * used_index[None, :], row_count)
    cos_rows = jnp.cos(row_angle)
    sin_rows = jnp.sin(row_angle)
    turn_angle = circle_angle(row_index[:, None] * col_index[None, :], padded_length)
    cos_turn = jnp.cos(turn_angle)
    sin_turn = jnp.sin(turn_angle)
    col_angle = circle_angle(col_index[:, None] * col_index[None, :], col_count)
    cos_cols = jnp.cos(col_angle)
    sin_cols = jnp.sin(col_angle)
    frequency = row_index[:, None] + row_count * col_index[None, :]
    group_size = math.gcd(local_channels, 16)
    group_count = local_channels // group_size
    mode_count = decay_time.shape[1]

    def one_group(parts):
        signal_part, time_part, residue_part = parts
        signal = signal_part.astype(jnp.float32)
        first_real = jnp.einsum("ka,cab->ckb", cos_rows, signal, precision=HIGHEST_PRECISION)
        first_imag = -jnp.einsum("ka,cab->ckb", sin_rows, signal, precision=HIGHEST_PRECISION)
        turned_real = first_real * cos_turn + first_imag * sin_turn
        turned_imag = first_imag * cos_turn - first_real * sin_turn
        freq_real = jnp.einsum(
            "ckb,bq->ckq", turned_real, cos_cols, precision=HIGHEST_PRECISION
        ) + jnp.einsum("ckb,bq->ckq", turned_imag, sin_cols, precision=HIGHEST_PRECISION)
        freq_imag = jnp.einsum(
            "ckb,bq->ckq", turned_imag, cos_cols, precision=HIGHEST_PRECISION
        ) - jnp.einsum("ckb,bq->ckq", turned_real, sin_cols, precision=HIGHEST_PRECISION)
        filt_real, filt_imag = filter_spectrum(
            time_part, residue_part, frequency, padded_length, sequence
        )
        prod_real = freq_real * filt_real - freq_imag * filt_imag
        prod_imag = freq_real * filt_imag + freq_imag * filt_real
        back_real = jnp.einsum(
            "ckq,bq->ckb", prod_real, cos_cols, precision=HIGHEST_PRECISION
        ) - jnp.einsum("ckq,bq->ckb", prod_imag, sin_cols, precision=HIGHEST_PRECISION)
        back_imag = jnp.einsum(
            "ckq,bq->ckb", prod_imag, cos_cols, precision=HIGHEST_PRECISION
        ) + jnp.einsum("ckq,bq->ckb", prod_real, sin_cols, precision=HIGHEST_PRECISION)
        spun_real = back_real * cos_turn - back_imag * sin_turn
        spun_imag = back_imag * cos_turn + back_real * sin_turn
        values = jnp.einsum(
            "ka,ckb->cab", cos_rows, spun_real, precision=HIGHEST_PRECISION
        ) - jnp.einsum("ka,ckb->cab", sin_rows, spun_imag, precision=HIGHEST_PRECISION)
        return (values / padded_length).astype(jnp.bfloat16)

    grouped_lines = lines.reshape(group_count, group_size, used_rows, col_count)
    time_groups = decay_time.reshape(group_count, group_size, mode_count)
    residue_groups = residue.reshape(group_count, group_size, mode_count)
    convolved = lax.map(one_group, (grouped_lines, time_groups, residue_groups))
    returned = lax.all_to_all(
        convolved.reshape(1, local_channels, sequence),
        "ctx",
        split_axis=2,
        concat_axis=0,
        tiled=True,
    )
    return jnp.transpose(returned.reshape(channels, length))


def local(activations, norm_gain, short_taps, skip_gain, time_const, residues):
    inputs = activations[0]
    length = inputs.shape[0]
    wide_in = inputs.astype(jnp.float32)
    square_mean = jnp.mean(wide_in * wide_in, axis=-1, keepdims=True)
    normed = (wide_in * lax.rsqrt(square_mean + 1e-06) * norm_gain[0].astype(jnp.float32)).astype(
        jnp.bfloat16
    )
    earlier_rows = from_behind(normed[length - 2 :], "ctx", 1)
    padded = jnp.concatenate([earlier_rows, normed], axis=0)
    wide_taps = short_taps[0].astype(jnp.float32)
    features = []
    for branch in range(3):
        total = jnp.zeros(inputs.shape, jnp.float32)
        for offset in range(3):
            total = total + wide_taps[branch, offset][None, :] * padded[
                2 - offset : 2 - offset + length
            ].astype(jnp.float32)
        features.append(total)
    query_feat, key_feat, value_feat = features
    mixed_in = (key_feat * value_feat).astype(jnp.bfloat16)
    conv_out = spectral_conv(mixed_in, time_const[0], residues[0])
    direct = skip_gain[0].astype(jnp.float32)[None, :] * mixed_in.astype(jnp.float32)
    block_out = (wide_in + query_feat * (conv_out.astype(jnp.float32) + direct)).astype(
        jnp.bfloat16
    )
    return from_behind_2(block_out[None], "phase", 1)


def solution(mesh):
    in_specs = (
        P("phase", "ctx", None),
        P("phase", None),
        P("phase", None, None, None),
        P("phase", None),
        P("phase", "ctx", None),
        P("phase", "ctx", None),
    )
    out_specs = P("phase", "ctx", None)
    return jax.shard_map(local, mesh=mesh, in_specs=in_specs, out_specs=out_specs, check_vma=False)
```

profile of v0, /device:TPU:1, one launch (start us, length us, event | category | flops | bytes accessed | tf_op | source)
XLA Modules:
  0.0 359.3 jit_solution(15073783701809906949)
XLA Ops:
  0.0 1.6 copy.105
  3.7 4.6 %collective-permute-start = (bf16[2,4096]{1,0:T(2,128)(2,1)S(1)}, bf16[2,4096]{1,0:T(2,128)(2,1)S(1)}, u32[]{:S(2)}, u32[]{:S(2)}) collective-permute-start(bf16[2,4096]{1,0:T(2,128)(2,1)S(1)} %copy.106), channel_id=1, source_target_pairs={{0,1},{1,2},{2,3},{3,4},{4,5},{5,6},{6,7},{7,8},{8,9},{9,10},{10,1... | collective-permute-start | bytes 49160 | tf_op jit(solution)/shard_map/ppermute | solution.py:14
  9.1 3.5 collective-permute-done
  13.1 5.6 %fusion.215 = bf16[128,4096]{0,1:T(8,128)(2,1)} fusion(bf16[128,4096]{0,1:T(8,128)(2,1)S(1)} %fusion.220, f32[4096]{0:T(1024)S(1)} %bitcast.389, f32[4096]{0:T(1024)S(1)} %bitcast.390, f32[4096]{0:T(1024)S(1)} %bitcast.391, f32[4096]{0:T(1024)S(1)} %bitcast.392, f32[4096]{0:T(1024)S(1)} %bitcast.393, f32[4096]{0:T(1024)S(1)} %bitcast.394, ...), kind=kLoop, calls=%fused_computation.400 | loop fusion | flops 11010048 | bytes 2211840 | tf_op jit(solution)/shard_map/convert_element_type | solution.py:142
  18.7 9.2 %all-to-all-start = ((bf16[64,64,128]{2,1,0:T(8,128)(2,1)}), bf16[64,64,128]{2,1,0:T(8,128)(2,1)}, u32[]{:S(2)}, u32[]{:S(2)}) async-start(bf16[64,64,128]{2,1,0:T(8,128)(2,1)} %bitcast.15), calls=%async_computation | async-start | bytes 2097152 | tf_op jit(solution)/shard_map/all_to_all | solution.py:55
  28.2 28.3 %all-to-all-done = bf16[64,64,128]{2,1,0:T(8,128)(2,1)} async-done(((bf16[64,64,128]{2,1,0:T(8,128)(2,1)}), bf16[64,64,128]{2,1,0:T(8,128)(2,1)}, u32[]{:S(2)}, u32[]{:S(2)}) %all-to-all-start) | async-done | bytes 1048608 | tf_op jit(solution)/shard_map/all_to_all | solution.py:55
  56.5 152.4 %while.18 = (s32[]{:T(128)}, bf16[4,16,64,128]{3,2,1,0:T(8,128)(2,1)}, bf16[4,16,64,128]{3,1,0,2:T(8,128)(2,1)}, f32[4,16,16]{1,0,2:T(4,128)S(1)}, f32[4,16,16]{1,0,2:T(4,128)S(1)}, /*index=5*/s32[128]{0:T(128)S(1)}, s32[]{:T(128)}) while((s32[]{:T(128)}, bf16[4,16,64,128]{3,2,1,0:T(8,128)(2,1)}, ...), condition=%wide.region_2.3_spmd.clone.clone.clone, body=%wide.region_1.2_spmd.clone.clone.clone.sunk | while | flops 4104389632 | bytes 44585556 | solution.py:111
  78.5 2.0 fusion.276
  80.5 2.0 convolution_add_fusion.4
  83.0 2.0 fusion.280
  85.6 12.2 %multiply_subtract_fusion.9 = (f32[16,128,128]{2,1,0:T(8,128)S(1)}, f32[16,128,128]{2,1,0:T(8,128)S(1)}, f32[16,128,128]{2,1,0:T(8,128)S(1)}, f32[16,128,128]{2,1,0:T(8,128)S(1)}) fusion(f32[16,128,128]{2,1,0:T(8,128)S(1)} %convolution_add_fusion.4, f32[16]{0:T(128)S(1)} %broadcast_multiply_fusion.32, f32[16]{0:T(128)S(1)} %get-tuple-element.1229, ...), kind=kOutput, calls=%fused_computation.108.clone.1 | convolution fusion | flops 471564288 | bytes 8721408 | tf_op jit(solution)/shard_map/while/body/eval_jaxpr/ckb,bq->ckq/dot_general | solution.py:89
  102.0 1.3 convolution_add_fusion.5
  103.3 1.5 fusion.283
  104.8 2.2 fusion.284
  109.8 2.0 fusion.276
  111.8 2.0 convolution_add_fusion.4
  114.3 2.0 fusion.280
  116.9 12.2 %multiply_subtract_fusion.9 = (f32[16,128,128]{2,1,0:T(8,128)S(1)}, f32[16,128,128]{2,1,0:T(8,128)S(1)}, f32[16,128,128]{2,1,0:T(8,128)S(1)}, f32[16,128,128]{2,1,0:T(8,128)S(1)}) fusion(f32[16,128,128]{2,1,0:T(8,128)S(1)} %convolution_add_fusion.4, f32[16]{0:T(128)S(1)} %broadcast_multiply_fusion.32, f32[16]{0:T(128)S(1)} %get-tuple-element.1229, ...), kind=kOutput, calls=%fused_computation.108.clone.1 | convolution fusion | flops 471564288 | bytes 8721408 | tf_op jit(solution)/shard_map/while/body/eval_jaxpr/ckb,bq->ckq/dot_general | solution.py:89
  133.4 1.3 convolution_add_fusion.5
  134.7 1.5 fusion.283
  136.1 2.2 fusion.284
  141.1 2.0 fusion.276
  143.1 2.0 convolution_add_fusion.4
  145.6 2.0 fusion.280
  148.3 12.2 %multiply_subtract_fusion.9 = (f32[16,128,128]{2,1,0:T(8,128)S(1)}, f32[16,128,128]{2,1,0:T(8,128)S(1)}, f32[16,128,128]{2,1,0:T(8,128)S(1)}, f32[16,128,128]{2,1,0:T(8,128)S(1)}) fusion(f32[16,128,128]{2,1,0:T(8,128)S(1)} %convolution_add_fusion.4, f32[16]{0:T(128)S(1)} %broadcast_multiply_fusion.32, f32[16]{0:T(128)S(1)} %get-tuple-element.1229, ...), kind=kOutput, calls=%fused_computation.108.clone.1 | convolution fusion | flops 471564288 | bytes 8721408 | tf_op jit(solution)/shard_map/while/body/eval_jaxpr/ckb,bq->ckq/dot_general | solution.py:89
  164.7 1.3 convolution_add_fusion.5
  166.0 1.5 fusion.283
  167.5 2.2 fusion.284
  172.4 2.0 fusion.276
  174.4 2.0 convolution_add_fusion.4
  176.9 2.0 fusion.280
  179.6 12.2 %multiply_subtract_fusion.9 = (f32[16,128,128]{2,1,0:T(8,128)S(1)}, f32[16,128,128]{2,1,0:T(8,128)S(1)}, f32[16,128,128]{2,1,0:T(8,128)S(1)}, f32[16,128,128]{2,1,0:T(8,128)S(1)}) fusion(f32[16,128,128]{2,1,0:T(8,128)S(1)} %convolution_add_fusion.4, f32[16]{0:T(128)S(1)} %broadcast_multiply_fusion.32, f32[16]{0:T(128)S(1)} %get-tuple-element.1229, ...), kind=kOutput, calls=%fused_computation.108.clone.1 | convolution fusion | flops 471564288 | bytes 8721408 | tf_op jit(solution)/shard_map/while/body/eval_jaxpr/ckb,bq->ckq/dot_general | solution.py:89
  193.4 1.3 convolution_subtract_fusion.4
  196.0 1.3 convolution_add_fusion.5
  197.3 1.5 fusion.283
  198.8 2.2 fusion.284
  208.9 1.5 reshape.1431
  210.4 6.8 %copy.111 = bf16[1,64,8192]{1,0,2:T(2,128)(2,1)} copy(bf16[1,64,8192]{2,1,0:T(8,128)(2,1)S(1)} %reshape.1431) | data formatting | bytes 2097152 | tf_op jit(solution)/shard_map/reshape | solution.py:113
  217.8 45.2 %reduce = bf16[8192,64]{1,0:T(8,128)(2,1)S(1)} reduce(bf16[8192,1,64]{2,1,0:T(2,128)(2,1)} %bitcast.378, bf16[]{:T(256)} %broadcast.1415), dimensions={1}, to_apply=%bitcast.256.reduce_sub_computation | reduce | bytes 2097154
  263.0 2.3 reshape.1506
  265.3 6.2 %all-to-all-start.1 = ((bf16[64,2,4096]{2,1,0:T(2,128)(2,1)}), bf16[64,2,4096]{2,1,0:T(2,128)(2,1)S(1)}, u32[]{:S(2)}, u32[]{:S(2)}) async-start(bf16[64,2,4096]{2,1,0:T(2,128)(2,1)} %reshape.1506), calls=%async_computation.1 | async-start | bytes 2097152 | tf_op jit(solution)/shard_map/all_to_all | solution.py:112
  271.5 28.5 %all-to-all-done.1 = bf16[64,2,4096]{2,1,0:T(2,128)(2,1)S(1)} async-done(((bf16[64,2,4096]{2,1,0:T(2,128)(2,1)}), bf16[64,2,4096]{2,1,0:T(2,128)(2,1)S(1)}, u32[]{:S(2)}, u32[]{:S(2)}) %all-to-all-start.1) | async-done | bytes 1048608 | tf_op jit(solution)/shard_map/all_to_all | solution.py:112
  300.1 7.0 %reshape.1507 = bf16[8192,1,64]{2,1,0:T(2,128)(2,1)} reshape(bf16[64,2,4096]{2,1,0:T(2,128)(2,1)S(1)} %all-to-all-done.1) | data formatting | bytes 2097152
  307.0 8.2 %copy.112 = bf16[1,64,8192]{2,1,0:T(8,128)(2,1)S(1)} copy(bf16[1,64,8192]{1,0,2:T(2,128)(2,1)} %bitcast.379) | data formatting | bytes 2097152 | tf_op jit(solution)/shard_map/all_to_all | solution.py:112
  317.6 6.1 %fusion.221 = bf16[128,4096]{0,1:T(8,128)(2,1)S(1)} fusion(bf16[128,4096]{0,1:T(8,128)(2,1)S(1)} %copy-done.3, f32[64,1,64,128]{3,2,0,1:T(8,128)S(1)} %copy.113, bf16[128,4096]{0,1:T(8,128)(2,1)} %fusion.215, bf16[1,128,4096]{1,2,0:T(8,128)(2,1)S(1)} %copy-done.1, f32[4096]{0:T(1024)S(1)} %bitcast.395, f32[4096]{0:T(1024)S(1)} %bitcast.387, ...), kind=kLoop, calls=%fused_computation.406 | loop fusion | flops 11010048 | bytes 6373376 | tf_op jit(solution)/shard_map/convert_element_type | solution.py:145
  323.7 4.0 %collective-permute-start.1 = (bf16[1,128,4096]{1,2,0:T(8,128)(2,1)S(1)}, bf16[1,128,4096]{1,2,0:T(8,128)(2,1)S(1)}, u32[]{:S(2)}, u32[]{:S(2)}) collective-permute-start(bf16[1,128,4096]{1,2,0:T(8,128)(2,1)S(1)} %bitcast.381), channel_id=1, source_target_pairs={{448,0},{0,64},{64,128},{128,192},{192,256},{256,320},{320,384},{3... | collective-permute-start | bytes 3145736 | tf_op jit(solution)/shard_map/ppermute | solution.py:20
  327.7 30.1 %collective-permute-done.1 = bf16[1,128,4096]{1,2,0:T(8,128)(2,1)S(1)} collective-permute-done((bf16[1,128,4096]{1,2,0:T(8,128)(2,1)S(1)}, bf16[1,128,4096]{1,2,0:T(8,128)(2,1)S(1)}, u32[]{:S(2)}, u32[]{:S(2)}) %collective-permute-start.1) | collective-permute-done | bytes 1048608 | tf_op jit(solution)/shard_map/ppermute | solution.py:20
  357.8 1.3 copy.114
  (225 shorter events, 36.3 us)
Async XLA Ops:
  0.0 2.2 copy-start.10
  1.6 1.7 copy-start
  3.0 10.1 %copy-start.2 = (bf16[128,4096]{0,1:T(8,128)(2,1)}, bf16[128,4096]{0,1:T(8,128)(2,1)S(1)}, u32[]{:S(2)}) copy-start(bf16[128,4096]{0,1:T(8,128)(2,1)S(1)} %fusion.220) | copy-start | bytes 3145732
  3.0 5.4 %copy-start.6 = (bf16[1,3,3,4096]{3,2,1,0:T(4,128)(2,1)S(1)}, bf16[1,3,3,4096]{3,2,1,0:T(4,128)(2,1)}, u32[]{:S(2)}) copy-start(bf16[1,3,3,4096]{3,2,1,0:T(4,128)(2,1)} %param.10) | copy-start | bytes 221188
  3.7 8.8 %collective-permute-start = (bf16[2,4096]{1,0:T(2,128)(2,1)S(1)}, bf16[2,4096]{1,0:T(2,128)(2,1)S(1)}, u32[]{:S(2)}, u32[]{:S(2)}) collective-permute-start(bf16[2,4096]{1,0:T(2,128)(2,1)S(1)} %copy.106), channel_id=1, source_target_pairs={{0,1},{1,2},{2,3},{3,4},{4,5},{5,6},{6,7},{7,8},{8,9},{9,10},{10,1... | collective-permute-start | bytes 49160 | tf_op jit(solution)/shard_map/ppermute | solution.py:14
  13.1 5.7 %copy-start.4 = (bf16[2,4096]{0,1:T(8,128)(2,1)}, bf16[2,4096]{0,1:T(8,128)(2,1)S(1)}, u32[]{:S(2)}) copy-start(bf16[2,4096]{0,1:T(8,128)(2,1)S(1)} %copy.107) | copy-start | bytes 49156
  13.1 14.9 %copy-start.12 = (f32[1,64,16]{1,2,0:T(8,128)S(1)}, f32[1,64,16]{1,2,0:T(8,128)}, u32[]{:S(2)}) copy-start(f32[1,64,16]{1,2,0:T(8,128)} %param.13) | copy-start | bytes 12292
  13.1 15.0 %copy-start.13 = (f32[1,64,16]{1,2,0:T(8,128)S(1)}, f32[1,64,16]{1,2,0:T(8,128)}, u32[]{:S(2)}) copy-start(f32[1,64,16]{1,2,0:T(8,128)} %param.12) | copy-start | bytes 12292
  18.7 37.7 %all-to-all-start = ((bf16[64,64,128]{2,1,0:T(8,128)(2,1)}), bf16[64,64,128]{2,1,0:T(8,128)(2,1)}, u32[]{:S(2)}, u32[]{:S(2)}) async-start(bf16[64,64,128]{2,1,0:T(8,128)(2,1)} %bitcast.15), calls=%async_computation | async-start | bytes 2097152 | tf_op jit(solution)/shard_map/all_to_all | solution.py:55
  263.0 8.5 %copy-start.11 = (bf16[1,4096]{1,0:T(2,128)(2,1)S(1)}, bf16[1,4096]{1,0:T(2,128)(2,1)}, u32[]{:S(2)}) copy-start(bf16[1,4096]{1,0:T(2,128)(2,1)} %param.11) | copy-start | bytes 24580
  265.3 34.8 %all-to-all-start.1 = ((bf16[64,2,4096]{2,1,0:T(2,128)(2,1)}), bf16[64,2,4096]{2,1,0:T(2,128)(2,1)S(1)}, u32[]{:S(2)}, u32[]{:S(2)}) async-start(bf16[64,2,4096]{2,1,0:T(2,128)(2,1)} %reshape.1506), calls=%async_computation.1 | async-start | bytes 2097152 | tf_op jit(solution)/shard_map/all_to_all | solution.py:112
  315.7 1.3 copy-start.1
  315.8 1.5 copy-start.3
  315.8 1.8 copy-start.5
  315.8 1.8 copy-start.7
  315.8 1.8 copy-start.8
  315.8 1.8 copy-start.9
  323.7 34.1 %collective-permute-start.1 = (bf16[1,128,4096]{1,2,0:T(8,128)(2,1)S(1)}, bf16[1,128,4096]{1,2,0:T(8,128)(2,1)S(1)}, u32[]{:S(2)}, u32[]{:S(2)}) collective-permute-start(bf16[1,128,4096]{1,2,0:T(8,128)(2,1)S(1)} %bitcast.381), channel_id=1, source_target_pairs={{448,0},{0,64},{64,128},{128,192},{192,256},{256,320},{320,384},{3... | collective-permute-start | bytes 3145736 | tf_op jit(solution)/shard_map/ppermute | solution.py:20
where the time goes:
time: 363 us; the launch traced here: 359 us
  matrix products  114 us (31%)
  waiting for transfers between devices  90.3 us (25%)
  other arithmetic  64.3 us (18%)
  local copies, waits for them, and re-layouts  37.6 us (10%)
  loops' own time  28.4 us (8%)
  starting transfers between devices  24.1 us (7%)
    dot_general x4, matrix products, one_group(): jnp.einsum('ckb,bq->ckq', turned_real, sin_cols, precision=HIGHEST_PRECIS...  48.8 us
    unnamed x2, other arithmetic  45.3 us
    ppermute x1, waiting for transfers between devices, from_behind_2(): return lax.ppermute(block, axis, route)  30.1 us
    all_to_all x1, waiting for transfers between devices, spectral_conv(): lax.all_to_all(convolved.reshape(1, local_channels, sequence), 'ctx', spl...  28.5 us
    another operation x1, loops' own time, spectral_conv(): convolved = lax.map(one_group, (grouped_lines, time_groups, residue_groups))  28.4 us
    all_to_all x1, waiting for transfers between devices, spectral_conv(): lax.all_to_all(pieces, 'ctx', split_axis=0, concat_axis=2, tiled=True)[0]  28.3 us
    unnamed x33, local copies, waits for them, and re-layouts  12.4 us
    all_to_all x1, starting transfers between devices, spectral_conv(): lax.all_to_all(pieces, 'ctx', split_axis=0, concat_axis=2, tiled=True)[0]  9.25 us
  transfers between devices with their start and end apart: 4, of which 4 were waited for; matrix products, arithmetic and copies ran while one was open for 0% of the time, Pallas kernels for 0%

commit v1 on v0

v1 whole, which is shorter than its diff:
```python
import functools

import jax
import jax.numpy as jnp
from jax import lax
from jax.experimental import pallas as pl
from jax.experimental.pallas import tpu as pltpu
from jax.sharding import PartitionSpec as P

MESH = pl.DeviceIdType.MESH
LANES = 128
MODES = 16
ROWS = 8
CORES = 2
F32 = jnp.float32
BF16 = jnp.bfloat16


def drain(ref, sem):
    pltpu.make_async_copy(ref, ref, sem).wait()


def kernel(
    phases, nx, tokens, act, prm, blk, out,
    halo, mate, raw, inv, par, rate, wgt, av, wv, qf, uu, ob,
    sb, rb, pb, cb, rt, rx,
    halo_sem, mate_sem, px_sem, py_sem, row_sem, tot_sem, car_sem, z_sem,
):
    nyc = ROWS * CORES
    ctx = nx * nyc
    groups = nx * ROWS
    channels = groups * LANES
    halves = nx // 2
    phase = lax.axis_index("phase")
    me = lax.axis_index("ctx")
    x = me // nyc
    yc = lax.rem(me, nyc)
    y = yc // CORES
    c = lax.rem(yc, CORES)
    after = lax.rem(me + 1, ctx)
    before = lax.rem(me + ctx - 1, ctx)
    above = lax.rem(phase + 1, phases)
    below = lax.rem(phase + phases - 1, phases)

    barrier = pltpu.get_barrier_semaphore()

    def greet_row(p, carry):
        peer = x * nyc + lax.rem(yc + p, nyc)
        pl.semaphore_signal(barrier, inc=1, device_id={"ctx": peer}, device_id_type=MESH)
        return carry

    lax.fori_loop(1, nyc, greet_row, 0)

    def greet_col(p, carry):
        peer = lax.rem(x + p, nx) * nyc + yc
        pl.semaphore_signal(barrier, inc=1, device_id={"ctx": peer}, device_id_type=MESH)
        return carry

    lax.fori_loop(1, nx, greet_col, 0)
    pl.semaphore_signal(barrier, inc=1, device_id={"ctx": before}, device_id_type=MESH)
    pl.semaphore_signal(barrier, inc=1, device_id={"phase": below}, device_id_type=MESH)
    pl.semaphore_wait(barrier, nyc - 1 + nx - 1 + 2)

    def send(src, dst, sems, where):
        pltpu.make_async_remote_copy(
            src_ref=src, dst_ref=dst, send_sem=sems.at[0], recv_sem=sems.at[1],
            device_id=where, device_id_type=MESH,
        ).start()

    def send_row(src, dst, sems):
        def one(p, carry):
            j = lax.rem(yc + p, nyc)
            send(src.at[pl.ds(j * MODES, MODES)], dst.at[pl.ds(yc * MODES, MODES)],
                 sems, {"ctx": x * nyc + j})
            return carry
        lax.fori_loop(1, nyc, one, 0)

    def send_col(src, dst, sems):
        def one(p, carry):
            peer = lax.rem(x + p, nx) * nyc + yc
            send(src, dst, sems, {"ctx": peer})
            return carry
        lax.fori_loop(1, nx, one, 0)

    send(blk, mate, mate_sem, {"ctx": x * nyc + y * CORES + (1 - c)})
    send(act.at[pl.ds(tokens - 16, 16)], halo, halo_sem, {"ctx": after})

    for g in range(groups):
        tile = prm[:, g * LANES:(g + 1) * LANES].astype(F32)
        par[pl.ds(g, 8, stride=groups), :] = tile[:8]
        par[pl.ds(8 * groups + g, 8, stride=groups), :] = tile[8:]

    drain(mate, mate_sem.at[1])
    slot = pl.ds((y * nx + x) * MODES, MODES)
    rate[slot, :] = blk[0:MODES, :] + mate[0:MODES, :]
    wgt[slot, :] = blk[MODES:2 * MODES, :] + mate[MODES:2 * MODES, :]
    send_col(rate.at[slot], rate.at[slot], px_sem.at[0])
    send_col(wgt.at[slot], wgt.at[slot], px_sem.at[1])

    def spread(tile_ref, source, place):
        total = jnp.zeros((16, LANES), F32)
        for g in range(groups):
            tile = tile_ref[pl.ds(source, 16), g * LANES:(g + 1) * LANES].astype(F32)
            raw[pl.ds(place * groups + g, 8, stride=groups), :] = tile[:8]
            raw[pl.ds((place + 8) * groups + g, 8, stride=groups), :] = tile[8:]
            total = total + tile * tile
        mean = jnp.sum(total, axis=1, keepdims=True) * (1.0 / channels)
        inv[pl.ds(place, 16), :] = jnp.broadcast_to(lax.rsqrt(mean + 1e-06), (16, LANES))

    def spread_own(i, carry):
        start = pl.multiple_of(i * 16, 16)
        spread(act, start, start + 16)
        return carry

    lax.fori_loop(0, tokens // 16, spread_own, 0)

    drain(rate.at[pl.ds(0, (nx - 1) * MODES)], px_sem.at[0, 1])
    drain(wgt.at[pl.ds(0, (nx - 1) * MODES)], px_sem.at[1, 1])
    line = pl.ds(y * nx * MODES, nx * MODES)

    def send_line(array, sems):
        def one(p, carry):
            peer = x * nyc + lax.rem(y + p, ROWS) * CORES + c
            send(array.at[line], array.at[line], sems, {"ctx": peer})
            return carry
        lax.fori_loop(1, ROWS, one, 0)

    send_line(rate, py_sem.at[0])
    send_line(wgt, py_sem.at[1])

    drain(halo, halo_sem.at[1])
    spread(halo, 0, 0)

    def rows_of(token, q):
        return pl.ds(pl.multiple_of(token * groups + 8 * q, 8), 8)

    first = jnp.where(me > 0, 1.0, 0.0).astype(F32)

    def features(q):
        gain = par[8 * q:8 * q + 8, :]
        taps = [par[(1 + j) * groups + 8 * q:(1 + j) * groups + 8 * q + 8, :] for j in range(9)]

        def normed(token):
            wide = raw[rows_of(token, q), :] * inv[pl.ds(token, 1), :] * gain
            return wide.astype(BF16).astype(F32)

        def one(i, carry):
            back1, back2 = carry
            for k in range(4):
                t = i * 4 + k
                now = normed(t + 16)
                feats = [
                    (taps[3 * b] * now + taps[3 * b + 1] * back1) + taps[3 * b + 2] * back2
                    for b in range(3)
                ]
                qf[rows_of(t, q), :] = feats[0]
                uu[rows_of(t, q), :] = (feats[1] * feats[2]).astype(BF16).astype(F32)
                back1, back2 = now, back1
            return back1, back2

        lax.fori_loop(0, tokens // 4, one, (normed(15) * first, normed(14) * first))

    for q in range(nx):
        features(q)

    drain(rate.at[pl.ds(0, (ROWS - 1) * nx * MODES)], py_sem.at[0, 1])
    for q in range(nx):
        for r in range(MODES):
            value = rate[pl.ds(q * MODES + r, 8, stride=nx * MODES), :]
            av[r * groups + 8 * q:r * groups + 8 * q + 8, :] = jnp.exp(-value)

    def end_state(h):
        for k in range(2):
            q = 2 * h + k
            decay = [av[r * groups + 8 * q:r * groups + 8 * q + 8, :] for r in range(MODES)]

            def one(i, state):
                for step in range(4):
                    value = uu[rows_of(i * 4 + step, q), :]
                    state = tuple(decay[r] * state[r] + value for r in range(MODES))
                return state

            state = lax.fori_loop(
                0, tokens // 4, one, tuple(jnp.zeros((8, LANES), F32) for _ in range(MODES))
            )
            for r in range(MODES):
                sb[h, pl.ds(k * MODES + r, 8, stride=CORES * MODES), :] = state[r]
        send_row(sb.at[h], rb.at[h], row_sem.at[h])
        own = pl.ds(yc * MODES, MODES)
        rb[h, own, :] = sb[h, own, :]

    for h in range(halves):
        end_state(h)

    def own_rate(h):
        return rate[pl.ds((y * nx + 2 * h + c) * MODES, MODES), :]

    for h in range(halves):
        drain(rb.at[h, pl.ds(0, (nyc - 1) * MODES)], row_sem.at[h, 1])
        shard_decay = jnp.exp(own_rate(h) * (-float(tokens)))
        state = jnp.zeros((MODES, LANES), F32)
        for j in range(nyc):
            pb[h, j * MODES:(j + 1) * MODES, :] = state
            state = shard_decay * state + rb[h, j * MODES:(j + 1) * MODES, :]
        rt[h] = state
        rx[h, pl.ds(x * MODES, MODES), :] = state
        send_col(rt.at[h], rx.at[h, pl.ds(x * MODES, MODES)], tot_sem.at[h])

    drain(wgt.at[pl.ds(0, (ROWS - 1) * nx * MODES)], py_sem.at[1, 1])
    for q in range(nx):
        for r in range(MODES):
            wv[r * groups + 8 * q:r * groups + 8 * q + 8, :] = (
                wgt[pl.ds(q * MODES + r, 8, stride=nx * MODES), :])

    for h in range(halves):
        drain(rx.at[h, pl.ds(0, (nx - 1) * MODES)], tot_sem.at[h, 1])
        shard_decay = jnp.exp(own_rate(h) * (-float(tokens)))
        line_decay = jnp.exp(own_rate(h) * (-float(tokens * nyc)))
        enter = jnp.zeros((MODES, LANES), F32)
        for k in range(nx):
            earlier = jnp.broadcast_to(jnp.where(k < x, 1.0, 0.0).astype(F32), (MODES, LANES))
            longer = line_decay * enter + rx[h, k * MODES:(k + 1) * MODES, :]
            enter = jnp.where(earlier > 0.5, longer, enter)
        for j in range(nyc):
            pb[h, j * MODES:(j + 1) * MODES, :] += enter
            enter = enter * shard_decay
        send_row(pb.at[h], cb.at[h], car_sem.at[h])
        own = pl.ds(yc * MODES, MODES)
        cb[h, own, :] = pb[h, own, :]

    def finish(h, k):
        q = 2 * h + k
        decay = [av[r * groups + 8 * q:r * groups + 8 * q + 8, :] for r in range(MODES)]
        weight = [wv[r * groups + 8 * q:r * groups + 8 * q + 8, :] for r in range(MODES)]
        skip = par[10 * groups + 8 * q:10 * groups + 8 * q + 8, :]

        def one(i, state):
            for step in range(4):
                t = i * 4 + step
                value = uu[rows_of(t, q), :]
                state = tuple(decay[r] * state[r] + value for r in range(MODES))
                terms = [weight[r] * state[r] for r in range(MODES)]
                while len(terms) > 1:
                    terms = [terms[2 * m] + terms[2 * m + 1] for m in range(len(terms) // 2)]
                conv = terms[0].astype(BF16).astype(F32)
                qf[rows_of(t, q), :] = (
                    raw[rows_of(t + 16, q), :]
                    + qf[rows_of(t, q), :] * (conv + skip * value))
            return state

        state = tuple(
            cb[h, pl.ds(k * MODES + r, 8, stride=CORES * MODES), :] for r in range(MODES))
        lax.fori_loop(0, tokens // 4, one, state)

        def gather(i, carry):
            start = pl.multiple_of(i * 16, 16)
            for g in range(8 * q, 8 * q + 8):
                low = qf[pl.ds(start * groups + g, 8, stride=groups), :]
                high = qf[pl.ds((start + 8) * groups + g, 8, stride=groups), :]
                ob[pl.ds(start, 16), g * LANES:(g + 1) * LANES] = (
                    jnp.concatenate([low, high], axis=0).astype(BF16))
            return carry

        lax.fori_loop(0, tokens // 16, gather, 0)
        part = pl.ds(q * 8 * LANES, 8 * LANES)
        send(ob.at[:, part], out.at[:, part], z_sem, {"phase": above})

    for h in range(halves):
        drain(cb.at[h, pl.ds(0, (nyc - 1) * MODES)], car_sem.at[h, 1])
        for k in range(2):
            finish(h, k)

    drain(blk, mate_sem.at[0])
    drain(halo, halo_sem.at[0])
    for k, array in enumerate((rate, wgt)):
        drain(array.at[pl.ds(0, (nx - 1) * MODES)], px_sem.at[k, 0])
        drain(array.at[pl.ds(0, (ROWS - 1) * nx * MODES)], py_sem.at[k, 0])
    for h in range(halves):
        drain(rb.at[h, pl.ds(0, (nyc - 1) * MODES)], row_sem.at[h, 0])
        drain(rx.at[h, pl.ds(0, (nx - 1) * MODES)], tot_sem.at[h, 0])
        drain(rb.at[h, pl.ds(0, (nyc - 1) * MODES)], car_sem.at[h, 0])
    drain(ob, z_sem.at[0])
    drain(ob, z_sem.at[1])


def local(phases, nx, activations, norm_gain, short_taps, skip_gain, time_const, residues):
    act = activations[0]
    tokens, channels = act.shape
    groups = channels // LANES
    halves = nx // 2
    nyc = ROWS * CORES
    prm = jnp.concatenate(
        [norm_gain, short_taps[0].reshape(9, channels), skip_gain,
         jnp.zeros((5, channels), BF16)], axis=0)
    rate = 1.0 / time_const[0]
    weight = residues[0] * jnp.sqrt(-jnp.expm1(-2.0 * rate))
    both = jnp.concatenate([rate.T, weight.T], axis=0)
    wide = jnp.concatenate([both, both], axis=1)
    half = LANES // CORES
    column = lax.broadcasted_iota(jnp.int32, wide.shape, 1) // half
    blk = jnp.where(column == lax.axis_index("ctx") % CORES, wide, 0.0)
    vmem = pltpu.VMEM
    dma = pltpu.SemaphoreType.DMA
    out = pl.pallas_call(
        functools.partial(kernel, phases, nx, tokens),
        out_shape=jax.ShapeDtypeStruct((tokens, channels), BF16),
        in_specs=[pl.BlockSpec(memory_space=vmem)] * 3,
        out_specs=pl.BlockSpec(memory_space=pl.ANY),
        scratch_shapes=[
            vmem((16, channels), BF16),
            vmem((2 * MODES, LANES), F32),
            vmem(((tokens + 16) * groups, LANES), F32),
            vmem((tokens + 16, LANES), F32),
            vmem((16 * groups, LANES), F32),
            vmem((groups * MODES, LANES), F32),
            vmem((groups * MODES, LANES), F32),
            vmem((groups * MODES, LANES), F32),
            vmem((groups * MODES, LANES), F32),
            vmem((tokens * groups, LANES), F32),
            vmem((tokens * groups, LANES), F32),
            vmem((tokens, channels), BF16),
            vmem((halves, nyc * MODES, LANES), F32),
            vmem((halves, nyc * MODES, LANES), F32),
            vmem((halves, nyc * MODES, LANES), F32),
            vmem((halves, nyc * MODES, LANES), F32),
            vmem((halves, MODES, LANES), F32),
            vmem((halves, nx * MODES, LANES), F32),
            dma((2,)),
            dma((2,)),
            dma((2, 2)),
            dma((2, 2)),
            dma((halves, 2)),
            dma((halves, 2)),
            dma((halves, 2)),
            dma((2,)),
        ],
        compiler_params=pltpu.CompilerParams(
            collective_id=0, has_side_effects=True, vmem_limit_bytes=40 * 1024 * 1024),
    )(act, prm, blk)
    return out[None]


def solution(mesh):
    in_specs = (
        P("phase", "ctx", None),
        P("phase", None),
        P("phase", None, None, None),
        P("phase", None),
        P("phase", "ctx", None),
        P("phase", "ctx", None),
    )
    nx = mesh.shape["ctx"] // (ROWS * CORES)
    return jax.shard_map(
        functools.partial(local, mesh.shape["phase"], nx),
        mesh=mesh, in_specs=in_specs, out_specs=P("phase", "ctx", None), check_vma=False)
```

time: 363 us -> 80.8 us (0.22)
  matrix products: 114 us -> 0 us
  waiting for transfers between devices: 90.3 us -> 0 us
  Pallas kernels: 0 us -> 75.7 us
  other arithmetic: 64.3 us -> 1.61 us
  local copies, waits for them, and re-layouts: 37.6 us -> 3.01 us
  loops' own time: 28.4 us -> 0 us
  starting transfers between devices: 24.1 us -> 0 us
    dot_general x48 -> x0, matrix products: 114 us -> none  [the longest x4 48.8 us: one_group(): jnp.einsum('ckb,bq->ckq', turned_real, sin_cols, precision=HIGHEST_PRECIS...]
    pallas_call x0 -> x1, Pallas kernels: none -> 75.7 us  [local(): pl.pallas_call(functools.partial(kernel, phases, nx, tokens), out_shape=j...]
    all_to_all x2 -> x0, waiting for transfers between devices: 56.8 us -> none  [the longest x1 28.5 us: spectral_conv(): lax.all_to_all(convolved.reshape(1, local_channels, sequence), 'ctx', spl...]
    unnamed x2 -> x0, other arithmetic: 45.3 us -> none
    ppermute x2 -> x0, waiting for transfers between devices: 33.6 us -> none  [the longest x1 30.1 us: from_behind_2(): return lax.ppermute(block, axis, route)]
    another operation x1 -> x0, loops' own time: 28.4 us -> none  [spectral_conv(): convolved = lax.map(one_group, (grouped_lines, time_groups, residue_groups))]
    all_to_all x2 -> x0, starting transfers between devices: 15.4 us -> none  [the longest x1 9.25 us: spectral_conv(): lax.all_to_all(pieces, 'ctx', split_axis=0, concat_axis=2, tiled=True)[0]]
    convert_element_type x8 -> x0, other arithmetic: 12.6 us -> none  [the longest x1 6.1 us: local(): (wide_in + query_feat * (conv_out.astype(jnp.float32) + direct)).astype(j...]
  transfers between devices with their start and end apart: 4 -> 0, of which waited for: 4 -> 0; matrix products, arithmetic and copies ran while one was open for 0% -> 0% of each run, Pallas kernels for 0% -> 0%
where the time goes in v1:
time: 80.8 us; the launch traced here: 80.4 us
  Pallas kernels  75.7 us (94%)
  local copies, waits for them, and re-layouts  3.01 us (4%)
  other arithmetic  1.61 us (2%)
    pallas_call x1, Pallas kernels, local(): pl.pallas_call(functools.partial(kernel, phases, nx, tokens), out_shape=j...  75.7 us
    unnamed x9, local copies, waits for them, and re-layouts  2.85 us

profile of v1, /device:TPU:1, one launch (start us, length us, event | category | flops | bytes accessed | tf_op | source)
XLA Modules:
  0.0 80.4 jit_solution(5085965245219971138)
XLA Ops:
  0.0 0.0 copy-start.1
  0.0 0.1 pad.7.clone
  0.1 0.7 fusion
  0.8 0.7 fusion.4
  1.5 0.1 maximum_select_fusion.blk
  1.6 0.0 copy-done.1
  1.6 0.0 copy-start.2
  1.6 0.0 copy-start.3
  1.6 0.1 reshape_squeeze.3
  1.7 0.6 copy-done.2
  2.3 0.0 copy-done.3
  2.4 0.1 maximum_maximum_fusion.prm
  2.5 0.0 copy-start
  2.5 1.2 %copy-done = bf16[1,128,4096]{2,1,0:T(8,128)(2,1)S(1)} copy-done((bf16[1,128,4096]{2,1,0:T(8,128)(2,1)S(1)}, bf16[1,128,4096]{2,1,0:T(8,128)(2,1)}, u32[]{:S(2)}) %copy-start) | copy-done | bytes 1048600
  3.7 75.7 %shard_map.64 = bf16[128,4096]{1,0:T(8,128)(2,1)S(1)} custom-call(bf16[128,4096]{1,0:T(8,128)(2,1)S(1)} %bitcast.22, bf16[16,4096]{1,0:T(8,128)(2,1)S(1)} %maximum_maximum_fusion.prm, f32[32,128]{1,0:T(8,128)S(1)} %maximum_select_fusion.blk), custom_call_target="tpu_custom_call" | custom-call | tf_op jit(solution)/shard_map/pallas_call | solution.py:304
  79.4 1.0 %copy.8 = bf16[1,128,4096]{2,1,0:T(8,128)(2,1)} copy(bf16[1,128,4096]{2,1,0:T(8,128)(2,1)S(1)} %bitcast.21) | data formatting | bytes 2097152
  (3 shorter events, 0.0 us)
Async XLA Ops:
  0.0 1.6 %copy-start.1 = (bf16[1,3,3,4096]{3,2,1,0:T(4,128)(2,1)S(1)}, bf16[1,3,3,4096]{3,2,1,0:T(4,128)(2,1)}, u32[]{:S(2)}) copy-start(bf16[1,3,3,4096]{3,2,1,0:T(4,128)(2,1)} %param.8) | copy-start | bytes 221188
  1.6 0.7 copy-start.2
  1.6 0.7 copy-start.3
  2.5 1.2 %copy-start = (bf16[1,128,4096]{2,1,0:T(8,128)(2,1)S(1)}, bf16[1,128,4096]{2,1,0:T(8,128)(2,1)}, u32[]{:S(2)}) copy-start(bf16[1,128,4096]{2,1,0:T(8,128)(2,1)} %param.6) | copy-start | bytes 3145732

commit v2 on v1

v2 whole, which is shorter than its diff:
```python
import functools

import jax
import jax.numpy as jnp
from jax import lax
from jax.experimental import pallas as pl
from jax.experimental.pallas import tpu as pltpu
from jax.sharding import PartitionSpec as P

MESH = pl.DeviceIdType.MESH
LANES = 128
MODES = 16
ROWS = 8
CORES = 2
NEAR = 1
PLAN = (
    (),
    ((2, 0, 128),),
    ((3, 0, 128),),
    (),
    (),
)
F32 = jnp.float32
BF16 = jnp.bfloat16


def drain(ref, sem):
    pltpu.make_async_copy(ref, ref, sem).wait()


def kernel(
    phases, nx, tokens, act, prm, blk, out,
    own, act_z, prm_z, halo, halo_z, mate, pair_z, both,
    raw_o, raw_z, inv_o, inv_z, par_o, par_z, uu_o, uu_z, qf_o, qf_z,
    first_rates, filt, av, wv, ob, sb, rb, pf, pb, cb, rt, rx,
    load_sem, halo_sem, mate_sem, pair_sem, prm_sem, act_sem, halo_z_sem, inv_z_sem,
    fy_sem, fx_sem, fs_sem, py_sem, px_sem, swap_sem,
    row_sem, tot_sem, car_sem, z_sem, store_sem,
):
    nyc = ROWS * CORES
    ctx = nx * nyc
    groups = nx * ROWS
    channels = groups * LANES
    halves = 2
    per = nx // halves
    near = NEAR * per
    few = MODES // CORES
    wide = ROWS * LANES
    phase = lax.axis_index("phase")
    me = lax.axis_index("ctx")
    x = me // nyc
    yc = lax.rem(me, nyc)
    y = yc // CORES
    c = lax.rem(yc, CORES)
    after = lax.rem(me + 1, ctx)
    before = lax.rem(me + ctx - 1, ctx)
    twin = x * nyc + y * CORES + (1 - c)
    above = lax.rem(phase + 1, phases)
    below = lax.rem(phase + phases - 1, phases)
    far = pl.ds(near * wide, channels - near * wide)

    load = pltpu.make_async_copy(act, own, load_sem)
    load.start()
    barrier = pltpu.get_barrier_semaphore()

    def greet(where):
        pl.semaphore_signal(barrier, inc=1, device_id=where, device_id_type=MESH)

    def greet_row(p, carry):
        greet({"ctx": x * nyc + lax.rem(yc + p, nyc)})
        return carry

    lax.fori_loop(1, nyc, greet_row, 0)

    def greet_col(p, carry):
        greet({"ctx": lax.rem(x + p, nx) * nyc + yc})
        return carry

    lax.fori_loop(1, nx, greet_col, 0)

    def greet_below(p, carry):
        greet({"phase": below, "ctx": x * nyc + p})
        return carry

    lax.fori_loop(0, nyc, greet_below, 0)
    greet({"ctx": before})
    greet({"phase": below, "ctx": before})

    def channel_rows(tile_ref, dest, g):
        tile = tile_ref[:, g * LANES:(g + 1) * LANES].astype(F32)
        dest[pl.ds(g, 8, stride=groups), :] = tile[:8]
        dest[pl.ds(8 * groups + g, 8, stride=groups), :] = tile[8:]

    for g in range(groups):
        channel_rows(prm, par_o, g)

    def place(dest, tile, at, g):
        dest[pl.ds(at * groups + g, 8, stride=groups), :] = tile[:8]
        dest[pl.ds((at + 8) * groups + g, 8, stride=groups), :] = tile[8:]

    def spread(tile_ref, source, at):
        total = jnp.zeros((16, LANES), F32)
        for g in range(groups):
            tile = tile_ref[pl.ds(source, 16), g * LANES:(g + 1) * LANES].astype(F32)
            place(raw_o, tile, at, g)
            total = total + tile * tile
        mean = jnp.sum(total, axis=1, keepdims=True) * (1.0 / channels)
        inv_o[pl.ds(at, 16), :] = jnp.broadcast_to(lax.rsqrt(mean + 1e-06), (16, LANES))

    def spread_own(i, carry):
        start = pl.multiple_of(i * 16, 16)
        spread(own, start, start + 16)
        return carry

    load.wait()
    lax.fori_loop(0, tokens // 16, spread_own, 0)

    pl.semaphore_wait(barrier, nyc - 1 + nx - 1 + nyc + 2)

    def send(src, dst, sems, where):
        pltpu.make_async_remote_copy(
            src_ref=src, dst_ref=dst, send_sem=sems.at[0], recv_sem=sems.at[1],
            device_id=where, device_id_type=MESH,
        ).start()

    def slot_of(j):
        return pl.ds(pl.multiple_of(j * MODES, MODES), MODES)

    def few_of(j):
        return pl.ds(pl.multiple_of(j * few, few), few)

    def send_row(src, dst, sems, up):
        def one(p, carry):
            j = lax.rem(yc + p, nyc)
            where = {"phase": above, "ctx": x * nyc + j} if up else {"ctx": x * nyc + j}
            send(src.at[slot_of(j)], dst.at[slot_of(yc)], sems, where)
            return carry
        lax.fori_loop(0 if up else 1, nyc, one, 0)

    def send_col(src, dst, sems):
        def one(p, carry):
            send(src, dst, sems, {"ctx": lax.rem(x + p, nx) * nyc + yc})
            return carry
        lax.fori_loop(1, nx, one, 0)

    def send_line(src, dst, sems):
        def one(p, carry):
            send(src, dst, sems, {"ctx": x * nyc + lax.rem(y + p, ROWS) * CORES + c})
            return carry
        lax.fori_loop(1, ROWS, one, 0)

    def send_act(q, start, count):
        part = pl.ds(q * wide, wide)
        rows = pl.ds(start, count)
        send(act.at[rows, part], act_z.at[rows, part], act_sem.at[q], {"phase": above})

    def send_acts(point):
        for q, start, count in PLAN[point]:
            if q >= near:
                send_act(q, start, count)

    send(blk, mate, mate_sem, {"ctx": twin})
    send(act.at[pl.ds(tokens - 16, 16)], halo, halo_sem, {"ctx": after})
    group = x * ROWS + y
    drain(mate, mate_sem.at[1])
    both[...] = blk[...] + mate[...]
    first_rates[c, few_of(group), :] = both[few_of(c), :]
    send_line(first_rates.at[c, few_of(group)], first_rates.at[c, few_of(group)], fy_sem)
    send(both.at[slot_of(c)], pair_z, pair_sem, {"phase": above})
    send(act.at[pl.ds(tokens - 16, 16), far], halo_z.at[:, far], halo_z_sem,
         {"phase": above, "ctx": after})
    send(inv_o.at[pl.ds(tokens, 16)], inv_z.at[pl.ds(0, 16)], inv_z_sem.at[1],
         {"phase": above, "ctx": after})
    send_acts(0)

    drain(halo, halo_sem.at[1])
    spread(halo, 0, 0)

    def rows_of(token, q):
        return pl.ds(pl.multiple_of(token * groups + 8 * q, 8), 8)

    def fixed(r, q):
        return slice(r * groups + 8 * q, r * groups + 8 * q + 8)

    first = jnp.where(me > 0, 1.0, 0.0).astype(F32)

    def features(q, raw, scale, par, uu, qf):
        gain = par[fixed(0, q), :]
        taps = [par[fixed(1 + j, q), :] for j in range(9)]

        def normed(token):
            value = raw[rows_of(token, q), :] * scale[pl.ds(token, 1), :] * gain
            return value.astype(BF16).astype(F32)

        def one(i, carry):
            back1, back2 = carry
            for k in range(4):
                t = i * 4 + k
                now = normed(t + 16)
                feats = [
                    None if b == 0 and qf is None else
                    (taps[3 * b] * now + taps[3 * b + 1] * back1) + taps[3 * b + 2] * back2
                    for b in range(3)
                ]
                if qf is not None:
                    qf[rows_of(t, q), :] = feats[0]
                uu[rows_of(t, q), :] = (feats[1] * feats[2]).astype(BF16).astype(F32)
                back1, back2 = now, back1
            return back1, back2

        lax.fori_loop(0, tokens // 4, one, (normed(15) * first, normed(14) * first))

    def features_own(q):
        features(q, raw_o, inv_o, par_o, uu_o, qf_o if q < near else None)

    for q in range(per):
        features_own(q)

    drain(first_rates.at[0, pl.ds(0, (ROWS - 1) * few)], fy_sem.at[1])
    line = pl.ds(pl.multiple_of(x * ROWS * few, ROWS * few), ROWS * few)
    send_col(first_rates.at[c, line], first_rates.at[c, line], fx_sem)

    drain(pair_z, pair_sem.at[1])
    home = jnp.broadcast_to(jnp.where(x < near, 1.0, 0.0).astype(F32), (MODES, LANES))
    filt[c, slot_of(group), :] = jnp.where(home > 0.5, both[slot_of(c), :], pair_z[...])
    send_line(filt.at[c, slot_of(group)], filt.at[c, slot_of(group)], py_sem)
    send_acts(1)

    for q in range(per, nx):
        features_own(q)

    drain(first_rates.at[0, pl.ds(0, (nx - 1) * ROWS * few)], fx_sem.at[1])
    send(first_rates.at[c], first_rates.at[c], fs_sem, {"ctx": twin})
    drain(first_rates.at[0], fs_sem.at[1])

    def end_state(h):
        for k in range(per):
            q = per * h + k
            decay = [
                jnp.exp(-first_rates[
                    r // few, pl.ds(q * ROWS * few + r % few, 8, stride=few), :])
                for r in range(MODES)
            ]
            for r in range(MODES):
                av[fixed(r, q), :] = decay[r]
            decay = [av[fixed(r, q), :] for r in range(MODES)]

            def one(i, state):
                for step in range(4):
                    value = uu_o[rows_of(i * 4 + step, q), :]
                    state = tuple(decay[r] * state[r] + value for r in range(MODES))
                return state

            state = lax.fori_loop(
                0, tokens // 4, one, tuple(jnp.zeros((8, LANES), F32) for _ in range(MODES))
            )
            for r in range(MODES):
                sb[h, pl.ds(k * MODES + r, 8, stride=CORES * MODES), :] = state[r]
        send_row(sb.at[h], rb.at[h], row_sem.at[h], False)
        rb[h, slot_of(yc), :] = sb[h, slot_of(yc), :]

    def own_rate(h):
        at = few_of((per * h + c) * ROWS + y)
        return jnp.concatenate([first_rates[0, at, :], first_rates[1, at, :]], axis=0)

    def line_sum(h):
        drain(rb.at[h, pl.ds(0, (nyc - 1) * MODES)], row_sem.at[h, 1])
        shard_decay = jnp.exp(own_rate(h) * (-float(tokens)))
        state = jnp.zeros((MODES, LANES), F32)
        for j in range(nyc):
            pf[h, j * MODES:(j + 1) * MODES, :] = state
            state = shard_decay * state + rb[h, j * MODES:(j + 1) * MODES, :]
        rt[h] = state
        rx[h, slot_of(x), :] = state
        send_col(rt.at[h], rx.at[h, slot_of(x)], tot_sem.at[h])

    def carries(h):
        drain(rx.at[h, pl.ds(0, (nx - 1) * MODES)], tot_sem.at[h, 1])
        shard_decay = jnp.exp(own_rate(h) * (-float(tokens)))
        line_decay = jnp.exp(own_rate(h) * (-float(tokens * nyc)))
        enter = jnp.zeros((MODES, LANES), F32)
        for k in range(nx):
            earlier = jnp.broadcast_to(jnp.where(k < x, 1.0, 0.0).astype(F32), (MODES, LANES))
            longer = line_decay * enter + rx[h, k * MODES:(k + 1) * MODES, :]
            enter = jnp.where(earlier > 0.5, longer, enter)
        for j in range(nyc):
            pb[h, j * MODES:(j + 1) * MODES, :] = pf[h, j * MODES:(j + 1) * MODES, :] + enter
            enter = enter * shard_decay
        send_row(pb.at[h], cb.at[h], car_sem.at[h], h >= NEAR)
        if h < NEAR:
            cb[h, slot_of(yc), :] = pb[h, slot_of(yc), :]

    def car_slots(h):
        return cb.at[h, pl.ds(0, (nyc if h >= NEAR else nyc - 1) * MODES)]

    def features_far(q):
        drain(act_z.at[:, pl.ds(q * wide, wide)], act_sem.at[q, 1])

        def spread_other(i, carry):
            start = pl.multiple_of(i * 16, 16)
            for g in range(8 * q, 8 * q + 8):
                tile = act_z[pl.ds(start, 16), g * LANES:(g + 1) * LANES].astype(F32)
                place(raw_z, tile, start + 16, g)
            return carry

        lax.fori_loop(0, tokens // 16, spread_other, 0)
        for g in range(8 * q, 8 * q + 8):
            place(raw_z, halo_z[:, g * LANES:(g + 1) * LANES].astype(F32), 0, g)
        features(q, raw_z, inv_z, par_z, uu_z, qf_z)

    def aligned(q):
        for r in range(MODES):
            at = pl.ds(q * ROWS * MODES + r, 8, stride=MODES)
            av[fixed(r, q), :] = jnp.exp(-filt[0, at, :])
            wv[fixed(r, q), :] = filt[1, at, :]

    def finish(h, k):
        q = per * h + k
        raw, uu, qf, par = (
            (raw_o, uu_o, qf_o, par_o) if q < near else (raw_z, uu_z, qf_z, par_z))
        decay = [av[fixed(r, q), :] for r in range(MODES)]
        weight = [wv[fixed(r, q), :] for r in range(MODES)]
        skip = par[fixed(10, q), :]

        def one(i, state):
            for step in range(4):
                t = i * 4 + step
                value = uu[rows_of(t, q), :]
                state = tuple(decay[r] * state[r] + value for r in range(MODES))
                terms = [weight[r] * state[r] for r in range(MODES)]
                while len(terms) > 1:
                    terms = [terms[2 * m] + terms[2 * m + 1] for m in range(len(terms) // 2)]
                conv = terms[0].astype(BF16).astype(F32)
                qf[rows_of(t, q), :] = (
                    raw[rows_of(t + 16, q), :]
                    + qf[rows_of(t, q), :] * (conv + skip * value))
            return state

        state = tuple(
            cb[h, pl.ds(k * MODES + r, 8, stride=CORES * MODES), :] for r in range(MODES))
        lax.fori_loop(0, tokens // 4, one, state)

        def gather(i, carry):
            start = pl.multiple_of(i * 16, 16)
            for g in range(8 * q, 8 * q + 8):
                low = qf[pl.ds(start * groups + g, 8, stride=groups), :]
                high = qf[pl.ds((start + 8) * groups + g, 8, stride=groups), :]
                ob[pl.ds(start, 16), g * LANES:(g + 1) * LANES] = (
                    jnp.concatenate([low, high], axis=0).astype(BF16))
            return carry

        lax.fori_loop(0, tokens // 16, gather, 0)
        part = pl.ds(q * wide, wide)
        if q < near:
            send(ob.at[:, part], out.at[:, part], z_sem, {"phase": above})
        else:
            pltpu.make_async_copy(ob.at[:, part], out.at[:, part], store_sem).start()

    end_state(0)
    end_state(1)
    drain(filt.at[0, pl.ds(0, (ROWS - 1) * MODES)], py_sem.at[1])
    span = pl.ds(pl.multiple_of(x * ROWS * MODES, ROWS * MODES), ROWS * MODES)
    send_col(filt.at[c, span], filt.at[c, span], px_sem)
    send(prm.at[:, far], prm_z.at[:, far], prm_sem, {"phase": above})
    send(inv_o.at[pl.ds(16, tokens)], inv_z.at[pl.ds(16, tokens)], inv_z_sem.at[0],
         {"phase": above})
    send_acts(2)
    line_sum(0)
    line_sum(1)
    send_acts(3)
    drain(filt.at[0, pl.ds(0, (nx - 1) * ROWS * MODES)], px_sem.at[1])
    send(filt.at[c], filt.at[c], swap_sem, {"ctx": twin})
    carries(0)
    carries(1)
    send_acts(4)
    drain(filt.at[0], swap_sem.at[1])
    for q in range(nx):
        aligned(q)
    drain(prm_z.at[:, far], prm_sem.at[1])
    for g in range(near * ROWS, groups):
        channel_rows(prm_z, par_z, g)
    drain(halo_z.at[:, far], halo_z_sem.at[1])
    drain(inv_z.at[pl.ds(16, tokens)], inv_z_sem.at[0, 1])
    drain(inv_z.at[pl.ds(0, 16)], inv_z_sem.at[1, 1])
    if NEAR == 0:
        features_far(0)
        features_far(1)
        drain(car_slots(0), car_sem.at[0, 1])
        finish(0, 0)
        finish(0, 1)
        features_far(2)
        drain(car_slots(1), car_sem.at[1, 1])
        finish(1, 0)
        features_far(3)
        finish(1, 1)
    else:
        drain(car_slots(0), car_sem.at[0, 1])
        finish(0, 0)
        finish(0, 1)
        features_far(2)
        features_far(3)
        drain(car_slots(1), car_sem.at[1, 1])
        finish(1, 0)
        finish(1, 1)

    drain(blk, mate_sem.at[0])
    drain(pair_z, pair_sem.at[0])
    drain(halo, halo_sem.at[0])
    drain(prm_z.at[:, far], prm_sem.at[0])
    for q in range(near, nx):
        drain(act_z.at[:, pl.ds(q * wide, wide)], act_sem.at[q, 0])
    drain(halo_z.at[:, far], halo_z_sem.at[0])
    drain(inv_z.at[pl.ds(16, tokens)], inv_z_sem.at[0, 0])
    drain(inv_z.at[pl.ds(0, 16)], inv_z_sem.at[1, 0])
    drain(first_rates.at[0, pl.ds(0, (ROWS - 1) * few)], fy_sem.at[0])
    drain(first_rates.at[0, pl.ds(0, (nx - 1) * ROWS * few)], fx_sem.at[0])
    drain(first_rates.at[0], fs_sem.at[0])
    drain(filt.at[0, pl.ds(0, (ROWS - 1) * MODES)], py_sem.at[0])
    drain(filt.at[0, pl.ds(0, (nx - 1) * ROWS * MODES)], px_sem.at[0])
    drain(filt.at[0], swap_sem.at[0])
    for h in range(halves):
        drain(rb.at[h, pl.ds(0, (nyc - 1) * MODES)], row_sem.at[h, 0])
        drain(rx.at[h, pl.ds(0, (nx - 1) * MODES)], tot_sem.at[h, 0])
        drain(car_slots(h), car_sem.at[h, 0])
    drain(ob.at[:, far], store_sem)
    if NEAR:
        drain(ob.at[:, pl.ds(0, near * wide)], z_sem.at[0])
        drain(ob.at[:, pl.ds(0, near * wide)], z_sem.at[1])


def local(phases, nx, activations, norm_gain, short_taps, skip_gain, time_const, residues):
    act = activations[0]
    tokens, channels = act.shape
    groups = channels // LANES
    halves = 2
    nyc = ROWS * CORES
    prm = jnp.concatenate(
        [norm_gain, short_taps[0].reshape(9, channels), skip_gain,
         jnp.zeros((5, channels), BF16)], axis=0)
    rate = 1.0 / time_const[0]
    weight = residues[0] * jnp.sqrt(-jnp.expm1(-2.0 * rate))
    both = jnp.concatenate([rate.T, weight.T], axis=0)
    wide = jnp.concatenate([both, both], axis=1)
    half = LANES // CORES
    column = lax.broadcasted_iota(jnp.int32, wide.shape, 1) // half
    blk = jnp.where(column == lax.axis_index("ctx") % CORES, wide, 0.0)
    vmem = pltpu.VMEM
    dma = pltpu.SemaphoreType.DMA
    out = pl.pallas_call(
        functools.partial(kernel, phases, nx, tokens),
        out_shape=jax.ShapeDtypeStruct((tokens, channels), BF16),
        in_specs=[
            pl.BlockSpec(memory_space=pl.ANY),
            pl.BlockSpec(memory_space=vmem),
            pl.BlockSpec(memory_space=vmem),
        ],
        out_specs=pl.BlockSpec(memory_space=pl.ANY),
        scratch_shapes=[
            vmem((tokens, channels), BF16),
            vmem((tokens, channels), BF16),
            vmem((16, channels), BF16),
            vmem((16, channels), BF16),
            vmem((16, channels), BF16),
            vmem((2 * MODES, LANES), F32),
            vmem((MODES, LANES), F32),
            vmem((2 * MODES, LANES), F32),
            vmem(((tokens + 16) * groups, LANES), F32),
            vmem(((tokens + 16) * groups, LANES), F32),
            vmem((tokens + 16, LANES), F32),
            vmem((tokens + 16, LANES), F32),
            vmem((16 * groups, LANES), F32),
            vmem((16 * groups, LANES), F32),
            vmem((tokens * groups, LANES), F32),
            vmem((tokens * groups, LANES), F32),
            vmem((tokens * groups, LANES), F32),
            vmem((tokens * groups, LANES), F32),
            vmem((CORES, groups * MODES // CORES, LANES), F32),
            vmem((2, groups * MODES, LANES), F32),
            vmem((groups * MODES, LANES), F32),
            vmem((groups * MODES, LANES), F32),
            vmem((tokens, channels), BF16),
            vmem((halves, nyc * MODES, LANES), F32),
            vmem((halves, nyc * MODES, LANES), F32),
            vmem((halves, nyc * MODES, LANES), F32),
            vmem((halves, nyc * MODES, LANES), F32),
            vmem((halves, nyc * MODES, LANES), F32),
            vmem((halves, MODES, LANES), F32),
            vmem((halves, nx * MODES, LANES), F32),
            dma(()),
            dma((2,)),
            dma((2,)),
            dma((2,)),
            dma((2,)),
            dma((nx, 2)),
            dma((2,)),
            dma((2, 2)),
            dma((2,)),
            dma((2,)),
            dma((2,)),
            dma((2,)),
            dma((2,)),
            dma((2,)),
            dma((halves, 2)),
            dma((halves, 2)),
            dma((halves, 2)),
            dma((2,)),
            dma(()),
        ],
        compiler_params=pltpu.CompilerParams(
            collective_id=0, has_side_effects=True, vmem_limit_bytes=56 * 1024 * 1024),
    )(act, prm, blk)
    return out[None]


def solution(mesh):
    in_specs = (
        P("phase", "ctx", None),
        P("phase", None),
        P("phase", None, None, None),
        P("phase", None),
        P("phase", "ctx", None),
        P("phase", "ctx", None),
    )
    nx = mesh.shape["ctx"] // (ROWS * CORES)
    return jax.shard_map(
        functools.partial(local, mesh.shape["phase"], nx),
        mesh=mesh, in_specs=in_specs, out_specs=P("phase", "ctx", None), check_vma=False)
```

time: 80.8 us -> 67.5 us (0.84)
  Pallas kernels: 75.7 us -> 60.8 us
  other arithmetic: 1.61 us -> 2.88 us
    pallas_call x1, Pallas kernels: 75.7 us -> 60.8 us  [local(): pl.pallas_call(functools.partial(kernel, phases, nx, tokens), out_shape=j...]
    unnamed x9 -> x7, local copies, waits for them, and re-layouts: 2.85 us -> 2.95 us
where the time goes in v2:
time: 67.5 us; the launch traced here: 66.8 us
  Pallas kernels  60.8 us (90%)
  local copies, waits for them, and re-layouts  3.1 us (5%)
  other arithmetic  2.88 us (4%)
    pallas_call x1, Pallas kernels, local(): pl.pallas_call(functools.partial(kernel, phases, nx, tokens), out_shape=j...  60.8 us
    unnamed x7, local copies, waits for them, and re-layouts  2.95 us
    transpose x2, other arithmetic, local(): both = jnp.concatenate([rate.T, weight.T], axis=0)  1.44 us

profile of v2, /device:TPU:1, one launch (start us, length us, event | category | flops | bytes accessed | tf_op | source)
XLA Modules:
  0.0 66.8 jit_solution(9872323044030897008)
XLA Ops:
  0.0 0.0 copy-start
  0.0 0.1 pad.7.clone
  0.1 0.7 %fusion = f32[16,64]{1,0:T(8,128)S(1)} fusion(f32[1,64,16]{1,2,0:T(8,128)} %param.11, f32[1,64,16]{1,2,0:T(8,128)} %param.10), kind=kLoop, calls=%fused_computation.4 | loop fusion | flops 4096 | bytes 12288 | tf_op jit(solution)/shard_map/transpose | solution.py:442
  0.8 0.7 %fusion.4 = f32[16,64]{1,0:T(8,128)S(1)} fusion(f32[1,64,16]{1,2,0:T(8,128)} %param.10), kind=kLoop, calls=%fused_computation.10 | loop fusion | flops 1024 | bytes 8192 | tf_op jit(solution)/shard_map/transpose | solution.py:442
  1.5 0.7 %maximum_select_fusion.blk = f32[32,128]{1,0:T(8,128)} fusion(f32[16,64]{1,0:T(8,128)S(1)} %fusion, f32[16,64]{1,0:T(8,128)S(1)} %fusion.4, s32[]{:T(128)S(6)} %select_n.17, s32[128]{0:T(128)S(1)} %get-tuple-element.5, s32[128]{0:T(128)S(1)} %get-tuple-element.6, pred[128]{0:T(512)(128)(4,1)S(1)} %compare_and_fusion), kind=kLoop, calls=%fused_computation.1 | loop fusion | flops 24576 | bytes 25732 | tf_op jit(solution)/shard_map/jit(_where)/select_n | solution.py:446
  2.2 0.0 copy-done
  2.2 0.0 copy-start.1
  2.2 0.0 copy-start.2
  2.2 0.1 reshape_squeeze.3
  2.3 0.6 copy-done.1
  3.0 0.0 copy-done.2
  3.0 0.7 %maximum_maximum_fusion.prm = bf16[16,4096]{1,0:T(8,128)(2,1)} fusion(bf16[1,4096]{1,0:T(2,128)(2,1)S(1)} %copy-done.1, bf16[9,4096]{1,0:T(8,128)(2,1)S(1)} %reshape_squeeze.3, bf16[1,4096]{1,0:T(2,128)(2,1)S(1)} %copy-done.2, bf16[16]{0:T(256)(128)(2,1)S(1)} %pad.7.clone), kind=kLoop, calls=%fused_computation | loop fusion | flops 524288 | bytes 221216 | tf_op jit(solution)/shard_map/concatenate | solution.py:437
  3.7 60.8 %shard_map.64 = bf16[128,4096]{1,0:T(8,128)(2,1)} custom-call(bf16[128,4096]{1,0:T(8,128)(2,1)} %bitcast.22, bf16[16,4096]{1,0:T(8,128)(2,1)} %maximum_maximum_fusion.prm, f32[32,128]{1,0:T(8,128)} %maximum_select_fusion.blk), custom_call_target="tpu_custom_call" | custom-call | tf_op jit(solution)/shard_map/pallas_call | solution.py:449
  64.5 2.3 %copy.8 = bf16[1,128,4096]{2,1,0:T(8,128)(2,1)} copy(bf16[1,128,4096]{2,1,0:T(8,128)(2,1)} %bitcast.21) | data formatting | bytes 2097152
  (3 shorter events, 0.0 us)
Async XLA Ops:
  0.0 2.2 %copy-start = (bf16[1,3,3,4096]{3,2,1,0:T(4,128)(2,1)S(1)}, bf16[1,3,3,4096]{3,2,1,0:T(4,128)(2,1)}, u32[]{:S(2)}) copy-start(bf16[1,3,3,4096]{3,2,1,0:T(4,128)(2,1)} %param.8) | copy-start | bytes 221188
  2.2 0.7 %copy-start.1 = (bf16[1,4096]{1,0:T(2,128)(2,1)S(1)}, bf16[1,4096]{1,0:T(2,128)(2,1)}, u32[]{:S(2)}) copy-start(bf16[1,4096]{1,0:T(2,128)(2,1)} %param.9) | copy-start | bytes 24580
  2.2 0.7 %copy-start.2 = (bf16[1,4096]{1,0:T(2,128)(2,1)S(1)}, bf16[1,4096]{1,0:T(2,128)(2,1)}, u32[]{:S(2)}) copy-start(bf16[1,4096]{1,0:T(2,128)(2,1)} %param.7) | copy-start | bytes 24580

commit v3 on v2

--- a/solution.py
+++ b/solution.py
@@ -12,14 +12,10 @@
 MODES = 16
 ROWS = 8
 CORES = 2
-NEAR = 1
-PLAN = (
-    (),
-    ((2, 0, 128),),
-    ((3, 0, 128),),
-    (),
-    (),
-)
+PARTS = ((0,), (1, 2, 3))
+EARLY = 1
+PLAN = (((1, 0, 128),), ((2, 0, 128),), ((3, 0, 128),), (), ())
+KINDS = 11
 F32 = jnp.float32
 BF16 = jnp.bfloat16
 
@@ -29,8 +25,8 @@
 
 
 def kernel(
-    phases, nx, tokens, act, prm, blk, out,
-    own, act_z, prm_z, halo, halo_z, mate, pair_z, both,
+    phases, nx, tokens, act, gains, taps_in, skips, tau, res, out,
+    blk, own, act_z, halo, halo_z, mate, pair_z, both,
     raw_o, raw_z, inv_o, inv_z, par_o, par_z, uu_o, uu_z, qf_o, qf_z,
     first_rates, filt, av, wv, ob, sb, rb, pf, pb, cb, rt, rx,
     load_sem, halo_sem, mate_sem, pair_sem, prm_sem, act_sem, halo_z_sem, inv_z_sem,
@@ -42,8 +38,7 @@
     groups = nx * ROWS
     channels = groups * LANES
     halves = 2
-    per = nx // halves
-    near = NEAR * per
+    near = len(PARTS[0])
     few = MODES // CORES
     wide = ROWS * LANES
     phase = lax.axis_index("phase")
@@ -86,13 +81,23 @@
     greet({"ctx": before})
     greet({"phase": below, "ctx": before})
 
-    def channel_rows(tile_ref, dest, g):
-        tile = tile_ref[:, g * LANES:(g + 1) * LANES].astype(F32)
-        dest[pl.ds(g, 8, stride=groups), :] = tile[:8]
-        dest[pl.ds(8 * groups + g, 8, stride=groups), :] = tile[8:]
+    rates = 1.0 / tau[...]
+    square = rates * rates
+    sinh = rates * (1.0 + square / 6.0 * (1.0 + square / 20.0 * (1.0 + square / 42.0)))
+    weights = res[...] * jnp.sqrt(2.0 * jnp.exp(-rates) * sinh)
+    half = LANES // CORES
+    for core in range(CORES):
+        this = jnp.where(c == core, 1.0, 0.0).astype(F32)
+        blk[0:MODES, core * half:(core + 1) * half] = rates * this
+        blk[MODES:2 * MODES, core * half:(core + 1) * half] = weights * this
 
     for g in range(groups):
-        channel_rows(prm, par_o, g)
+        lanes = slice(g * LANES, (g + 1) * LANES)
+        base = g // 8 * KINDS * 8 + g % 8
+        par_o[base:base + 1, :] = gains[:, lanes].astype(F32)
+        for b in range(3):
+            par_o[pl.ds(base + (1 + 3 * b) * 8, 3, stride=8), :] = taps_in[b, :, lanes].astype(F32)
+        par_o[base + 80:base + 81, :] = skips[:, lanes].astype(F32)
 
     def place(dest, tile, at, g):
         dest[pl.ds(at * groups + g, 8, stride=groups), :] = tile[:8]
@@ -129,11 +134,16 @@
     def few_of(j):
         return pl.ds(pl.multiple_of(j * few, few), few)
 
-    def send_row(src, dst, sems, up):
+    deep = [len(quarters) * few for quarters in PARTS]
+
+    def deep_of(h, j):
+        return pl.ds(pl.multiple_of(j * deep[h], few), deep[h])
+
+    def send_row(h, src, dst, sems, up):
         def one(p, carry):
             j = lax.rem(yc + p, nyc)
             where = {"phase": above, "ctx": x * nyc + j} if up else {"ctx": x * nyc + j}
-            send(src.at[slot_of(j)], dst.at[slot_of(yc)], sems, where)
+            send(src.at[deep_of(h, j)], dst.at[deep_of(h, yc)], sems, where)
             return carry
         lax.fori_loop(0 if up else 1, nyc, one, 0)
 
@@ -182,11 +192,15 @@
     def fixed(r, q):
         return slice(r * groups + 8 * q, r * groups + 8 * q + 8)
 
+    def param(j, q):
+        return slice((q * KINDS + j) * 8, (q * KINDS + j) * 8 + 8)
+
+    far_par = pl.ds(near * KINDS * 8, (nx - near) * KINDS * 8)
     first = jnp.where(me > 0, 1.0, 0.0).astype(F32)
 
     def features(q, raw, scale, par, uu, qf):
-        gain = par[fixed(0, q), :]
-        taps = [par[fixed(1 + j, q), :] for j in range(9)]
+        gain = par[param(0, q), :]
+        taps = [par[param(1 + j, q), :] for j in range(9)]
 
         def normed(token):
             value = raw[rows_of(token, q), :] * scale[pl.ds(token, 1), :] * gain
@@ -213,7 +227,7 @@
     def features_own(q):
         features(q, raw_o, inv_o, par_o, uu_o, qf_o if q < near else None)
 
-    for q in range(per):
+    for q in PARTS[0]:
         features_own(q)
 
     drain(first_rates.at[0, pl.ds(0, (ROWS - 1) * few)], fy_sem.at[1])
@@ -226,16 +240,18 @@
     send_line(filt.at[c, slot_of(group)], filt.at[c, slot_of(group)], py_sem)
     send_acts(1)
 
-    for q in range(per, nx):
+    for q in PARTS[1]:
         features_own(q)
 
     drain(first_rates.at[0, pl.ds(0, (nx - 1) * ROWS * few)], fx_sem.at[1])
     send(first_rates.at[c], first_rates.at[c], fs_sem, {"ctx": twin})
     drain(first_rates.at[0], fs_sem.at[1])
 
+    def strided(h, k, r):
+        return pl.ds(r // few * deep[h] + k * few + r % few, 8, stride=CORES * deep[h])
+
     def end_state(h):
-        for k in range(per):
-            q = per * h + k
+        for k, q in enumerate(PARTS[h]):
             decay = [
                 jnp.exp(-first_rates[
                     r // few, pl.ds(q * ROWS * few + r % few, 8, stride=few), :])
@@ -255,43 +271,43 @@
                 0, tokens // 4, one, tuple(jnp.zeros((8, LANES), F32) for _ in range(MODES))
             )
             for r in range(MODES):
-                sb[h, pl.ds(k * MODES + r, 8, stride=CORES * MODES), :] = state[r]
-        send_row(sb.at[h], rb.at[h], row_sem.at[h], False)
-        rb[h, slot_of(yc), :] = sb[h, slot_of(yc), :]
+                sb[h, strided(h, k, r), :] = state[r]
+        send_row(h, sb.at[h], rb.at[h], row_sem.at[h], False)
+        rb[h, deep_of(h, yc), :] = sb[h, deep_of(h, yc), :]
 
     def own_rate(h):
-        at = few_of((per * h + c) * ROWS + y)
-        return jnp.concatenate([first_rates[0, at, :], first_rates[1, at, :]], axis=0)
+        return jnp.concatenate(
+            [first_rates[c, few_of(q * ROWS + y), :] for q in PARTS[h]], axis=0)
 
     def line_sum(h):
-        drain(rb.at[h, pl.ds(0, (nyc - 1) * MODES)], row_sem.at[h, 1])
+        drain(rb.at[h, pl.ds(0, (nyc - 1) * deep[h])], row_sem.at[h, 1])
         shard_decay = jnp.exp(own_rate(h) * (-float(tokens)))
-        state = jnp.zeros((MODES, LANES), F32)
+        state = jnp.zeros((deep[h], LANES), F32)
         for j in range(nyc):
-            pf[h, j * MODES:(j + 1) * MODES, :] = state
-            state = shard_decay * state + rb[h, j * MODES:(j + 1) * MODES, :]
-        rt[h] = state
-        rx[h, slot_of(x), :] = state
-        send_col(rt.at[h], rx.at[h, slot_of(x)], tot_sem.at[h])
+            pf[h, j * deep[h]:(j + 1) * deep[h], :] = state
+            state = shard_decay * state + rb[h, j * deep[h]:(j + 1) * deep[h], :]
+        rt[h, 0:deep[h], :] = state
+        rx[h, deep_of(h, x), :] = state
+        send_col(rt.at[h, pl.ds(0, deep[h])], rx.at[h, deep_of(h, x)], tot_sem.at[h])
 
     def carries(h):
-        drain(rx.at[h, pl.ds(0, (nx - 1) * MODES)], tot_sem.at[h, 1])
+        drain(rx.at[h, pl.ds(0, (nx - 1) * deep[h])], tot_sem.at[h, 1])
         shard_decay = jnp.exp(own_rate(h) * (-float(tokens)))
         line_decay = jnp.exp(own_rate(h) * (-float(tokens * nyc)))
-        enter = jnp.zeros((MODES, LANES), F32)
+        enter = jnp.zeros((deep[h], LANES), F32)
         for k in range(nx):
-            earlier = jnp.broadcast_to(jnp.where(k < x, 1.0, 0.0).astype(F32), (MODES, LANES))
-            longer = line_decay * enter + rx[h, k * MODES:(k + 1) * MODES, :]
+            earlier = jnp.broadcast_to(jnp.where(k < x, 1.0, 0.0).astype(F32), (deep[h], LANES))
+            longer = line_decay * enter + rx[h, k * deep[h]:(k + 1) * deep[h], :]
             enter = jnp.where(earlier > 0.5, longer, enter)
         for j in range(nyc):
-            pb[h, j * MODES:(j + 1) * MODES, :] = pf[h, j * MODES:(j + 1) * MODES, :] + enter
+            pb[h, j * deep[h]:(j + 1) * deep[h], :] = pf[h, j * deep[h]:(j + 1) * deep[h], :] + enter
             enter = enter * shard_decay
-        send_row(pb.at[h], cb.at[h], car_sem.at[h], h >= NEAR)
-        if h < NEAR:
-            cb[h, slot_of(yc), :] = pb[h, slot_of(yc), :]
+        send_row(h, pb.at[h], cb.at[h], car_sem.at[h], h > 0)
+        if h == 0:
+            cb[h, deep_of(h, yc), :] = pb[h, deep_of(h, yc), :]
 
     def car_slots(h):
-        return cb.at[h, pl.ds(0, (nyc if h >= NEAR else nyc - 1) * MODES)]
+        return cb.at[h, pl.ds(0, (nyc if h > 0 else nyc - 1) * deep[h])]
 
     def features_far(q):
         drain(act_z.at[:, pl.ds(q * wide, wide)], act_sem.at[q, 1])
@@ -315,12 +331,12 @@
             wv[fixed(r, q), :] = filt[1, at, :]
 
     def finish(h, k):
-        q = per * h + k
+        q = PARTS[h][k]
         raw, uu, qf, par = (
             (raw_o, uu_o, qf_o, par_o) if q < near else (raw_z, uu_z, qf_z, par_z))
         decay = [av[fixed(r, q), :] for r in range(MODES)]
         weight = [wv[fixed(r, q), :] for r in range(MODES)]
-        skip = par[fixed(10, q), :]
+        skip = par[param(10, q), :]
 
         def one(i, state):
             for step in range(4):
@@ -337,7 +353,7 @@
             return state
 
         state = tuple(
-            cb[h, pl.ds(k * MODES + r, 8, stride=CORES * MODES), :] for r in range(MODES))
+            cb[h, strided(h, k, r), :] for r in range(MODES))
         lax.fori_loop(0, tokens // 4, one, state)
 
         def gather(i, carry):
@@ -361,7 +377,7 @@
     drain(filt.at[0, pl.ds(0, (ROWS - 1) * MODES)], py_sem.at[1])
     span = pl.ds(pl.multiple_of(x * ROWS * MODES, ROWS * MODES), ROWS * MODES)
     send_col(filt.at[c, span], filt.at[c, span], px_sem)
-    send(prm.at[:, far], prm_z.at[:, far], prm_sem, {"phase": above})
+    send(par_o.at[far_par], par_z.at[far_par], prm_sem, {"phase": above})
     send(inv_o.at[pl.ds(16, tokens)], inv_z.at[pl.ds(16, tokens)], inv_z_sem.at[0],
          {"phase": above})
     send_acts(2)
@@ -376,37 +392,25 @@
     drain(filt.at[0], swap_sem.at[1])
     for q in range(nx):
         aligned(q)
-    drain(prm_z.at[:, far], prm_sem.at[1])
-    for g in range(near * ROWS, groups):
-        channel_rows(prm_z, par_z, g)
+    drain(par_z.at[far_par], prm_sem.at[1])
     drain(halo_z.at[:, far], halo_z_sem.at[1])
     drain(inv_z.at[pl.ds(16, tokens)], inv_z_sem.at[0, 1])
     drain(inv_z.at[pl.ds(0, 16)], inv_z_sem.at[1, 1])
-    if NEAR == 0:
-        features_far(0)
-        features_far(1)
-        drain(car_slots(0), car_sem.at[0, 1])
-        finish(0, 0)
-        finish(0, 1)
-        features_far(2)
-        drain(car_slots(1), car_sem.at[1, 1])
-        finish(1, 0)
-        features_far(3)
-        finish(1, 1)
-    else:
-        drain(car_slots(0), car_sem.at[0, 1])
-        finish(0, 0)
-        finish(0, 1)
-        features_far(2)
-        features_far(3)
-        drain(car_slots(1), car_sem.at[1, 1])
-        finish(1, 0)
-        finish(1, 1)
+    for q in PARTS[1][:EARLY]:
+        features_far(q)
+    drain(car_slots(0), car_sem.at[0, 1])
+    for k in range(len(PARTS[0])):
+        finish(0, k)
+    for q in PARTS[1][EARLY:]:
+        features_far(q)
+    drain(car_slots(1), car_sem.at[1, 1])
+    for k in range(len(PARTS[1])):
+        finish(1, k)
 
     drain(blk, mate_sem.at[0])
     drain(pair_z, pair_sem.at[0])
     drain(halo, halo_sem.at[0])
-    drain(prm_z.at[:, far], prm_sem.at[0])
+    drain(par_z.at[far_par], prm_sem.at[0])
     for q in range(near, nx):
         drain(act_z.at[:, pl.ds(q * wide, wide)], act_sem.at[q, 0])
     drain(halo_z.at[:, far], halo_z_sem.at[0])
@@ -419,13 +423,12 @@
     drain(filt.at[0, pl.ds(0, (nx - 1) * ROWS * MODES)], px_sem.at[0])
     drain(filt.at[0], swap_sem.at[0])
     for h in range(halves):
-        drain(rb.at[h, pl.ds(0, (nyc - 1) * MODES)], row_sem.at[h, 0])
-        drain(rx.at[h, pl.ds(0, (nx - 1) * MODES)], tot_sem.at[h, 0])
+        drain(rb.at[h, pl.ds(0, (nyc - 1) * deep[h])], row_sem.at[h, 0])
+        drain(rx.at[h, pl.ds(0, (nx - 1) * deep[h])], tot_sem.at[h, 0])
         drain(car_slots(h), car_sem.at[h, 0])
     drain(ob.at[:, far], store_sem)
-    if NEAR:
-        drain(ob.at[:, pl.ds(0, near * wide)], z_sem.at[0])
-        drain(ob.at[:, pl.ds(0, near * wide)], z_sem.at[1])
+    drain(ob.at[:, pl.ds(0, near * wide)], z_sem.at[0])
+    drain(ob.at[:, pl.ds(0, near * wide)], z_sem.at[1])
 
 
 def local(phases, nx, activations, norm_gain, short_taps, skip_gain, time_const, residues):
@@ -434,16 +437,7 @@
     groups = channels // LANES
     halves = 2
     nyc = ROWS * CORES
-    prm = jnp.concatenate(
-        [norm_gain, short_taps[0].reshape(9, channels), skip_gain,
-         jnp.zeros((5, channels), BF16)], axis=0)
-    rate = 1.0 / time_const[0]
-    weight = residues[0] * jnp.sqrt(-jnp.expm1(-2.0 * rate))
-    both = jnp.concatenate([rate.T, weight.T], axis=0)
-    wide = jnp.concatenate([both, both], axis=1)
-    half = LANES // CORES
-    column = lax.broadcasted_iota(jnp.int32, wide.shape, 1) // half
-    blk = jnp.where(column == lax.axis_index("ctx") % CORES, wide, 0.0)
+    most = max(len(quarters) for quarters in PARTS) * MODES // CORES
     vmem = pltpu.VMEM
     dma = pltpu.SemaphoreType.DMA
     out = pl.pallas_call(
@@ -453,12 +447,15 @@
             pl.BlockSpec(memory_space=pl.ANY),
             pl.BlockSpec(memory_space=vmem),
             pl.BlockSpec(memory_space=vmem),
+            pl.BlockSpec(memory_space=vmem),
+            pl.BlockSpec(memory_space=vmem),
+            pl.BlockSpec(memory_space=vmem),
         ],
         out_specs=pl.BlockSpec(memory_space=pl.ANY),
         scratch_shapes=[
+            vmem((2 * MODES, LANES), F32),
             vmem((tokens, channels), BF16),
             vmem((tokens, channels), BF16),
-            vmem((16, channels), BF16),
             vmem((16, channels), BF16),
             vmem((16, channels), BF16),
             vmem((2 * MODES, LANES), F32),
@@ -468,8 +465,8 @@
             vmem(((tokens + 16) * groups, LANES), F32),
             vmem((tokens + 16, LANES), F32),
             vmem((tokens + 16, LANES), F32),
-            vmem((16 * groups, LANES), F32),
-            vmem((16 * groups, LANES), F32),
+            vmem((KINDS * groups, LANES), F32),
+            vmem((KINDS * groups, LANES), F32),
             vmem((tokens * groups, LANES), F32),
             vmem((tokens * groups, LANES), F32),
             vmem((tokens * groups, LANES), F32),
@@ -479,13 +476,13 @@
             vmem((groups * MODES, LANES), F32),
             vmem((groups * MODES, LANES), F32),
             vmem((tokens, channels), BF16),
-            vmem((halves, nyc * MODES, LANES), F32),
-            vmem((halves, nyc * MODES, LANES), F32),
-            vmem((halves, nyc * MODES, LANES), F32),
-            vmem((halves, nyc * MODES, LANES), F32),
-            vmem((halves, nyc * MODES, LANES), F32),
-            vmem((halves, MODES, LANES), F32),
-            vmem((halves, nx * MODES, LANES), F32),
+            vmem((halves, nyc * most, LANES), F32),
+            vmem((halves, nyc * most, LANES), F32),
+            vmem((halves, nyc * most, LANES), F32),
+            vmem((halves, nyc * most, LANES), F32),
+            vmem((halves, nyc * most, LANES), F32),
+            vmem((halves, most, LANES), F32),
+            vmem((halves, nx * most, LANES), F32),
             dma(()),
             dma((2,)),
             dma((2,)),
@@ -508,7 +505,7 @@
         ],
         compiler_params=pltpu.CompilerParams(
             collective_id=0, has_side_effects=True, vmem_limit_bytes=56 * 1024 * 1024),
-    )(act, prm, blk)
+    )(act, norm_gain, short_taps[0], skip_gain, time_const[0].T, residues[0].T)
     return out[None]
 
 

time: 67.5 us -> 59.2 us (0.88)
  Pallas kernels: 60.8 us -> 56.7 us
  other arithmetic: 2.88 us -> 0 us
  local copies, waits for them, and re-layouts: 3.1 us -> 2.29 us
    pallas_call x1, Pallas kernels: 60.8 us -> 56.7 us  [local(): pl.pallas_call(functools.partial(kernel, phases, nx, tokens), out_shape=j...]
    transpose x2 -> x0, other arithmetic: 1.44 us -> none  [local(): both = jnp.concatenate([rate.T, weight.T], axis=0)]
    concatenate x1 -> x0, other arithmetic: 0.74 us -> none  [local(): jnp.concatenate([norm_gain, short_taps[0].reshape(9, channels), skip_gain...]
    select_n x1 -> x0, other arithmetic: 0.69 us -> none  [local(): blk = jnp.where(column == lax.axis_index('ctx') % CORES, wide, 0.0)]
    unnamed x7 -> x1, local copies, waits for them, and re-layouts: 2.95 us -> 2.29 us
where the time goes in v3:
time: 59.2 us; the launch traced here: 59 us
  Pallas kernels  56.7 us (96%)
  local copies, waits for them, and re-layouts  2.29 us (4%)
    pallas_call x1, Pallas kernels, local(): pl.pallas_call(functools.partial(kernel, phases, nx, tokens), out_shape=j...  56.7 us
    unnamed x1, local copies, waits for them, and re-layouts  2.29 us

profile of v3, /device:TPU:1, one launch (start us, length us, event | category | flops | bytes accessed | tf_op | source)
XLA Modules:
  0.0 59.0 jit_solution(4029200404668291861)
XLA Ops:
  0.0 56.7 %shard_map.64 = bf16[128,4096]{1,0:T(8,128)(2,1)} custom-call(bf16[128,4096]{1,0:T(8,128)(2,1)} %bitcast.10, bf16[1,4096]{1,0:T(2,128)(2,1)} %gains.1, bf16[3,3,4096]{2,1,0:T(4,128)(2,1)} %bitcast.11, bf16[1,4096]{1,0:T(2,128)(2,1)} %skips.1, f32[16,64]{1,0:T(8,128)} %bitcast.12, f32[16,64]{1,0:T(8,128)} %bitcast.13), custom_call_target="tpu_custom_call" | custom-call | tf_op jit(solution)/shard_map/pallas_call | solution.py:443
  56.7 2.3 %copy.8 = bf16[1,128,4096]{2,1,0:T(8,128)(2,1)} copy(bf16[1,128,4096]{2,1,0:T(8,128)(2,1)} %bitcast.9) | data formatting | bytes 2097152

commit v4 on v3

--- a/solution.py
+++ b/solution.py
@@ -139,23 +139,26 @@
     def deep_of(h, j):
         return pl.ds(pl.multiple_of(j * deep[h], few), deep[h])
 
+    def far_first(k, count):
+        return count // 2 + (1 - 2 * lax.rem(k, 2)) * (k // 2)
+
     def send_row(h, src, dst, sems, up):
         def one(p, carry):
-            j = lax.rem(yc + p, nyc)
+            j = lax.rem(yc + far_first(p, nyc), nyc)
             where = {"phase": above, "ctx": x * nyc + j} if up else {"ctx": x * nyc + j}
             send(src.at[deep_of(h, j)], dst.at[deep_of(h, yc)], sems, where)
             return carry
-        lax.fori_loop(0 if up else 1, nyc, one, 0)
+        lax.fori_loop(1, nyc + 1 if up else nyc, one, 0, unroll=True)
 
     def send_col(src, dst, sems):
         def one(p, carry):
-            send(src, dst, sems, {"ctx": lax.rem(x + p, nx) * nyc + yc})
+            send(src, dst, sems, {"ctx": lax.rem(x + far_first(p, nx), nx) * nyc + yc})
             return carry
         lax.fori_loop(1, nx, one, 0)
 
     def send_line(src, dst, sems):
         def one(p, carry):
-            send(src, dst, sems, {"ctx": x * nyc + lax.rem(y + p, ROWS) * CORES + c})
+            send(src, dst, sems, {"ctx": x * nyc + lax.rem(y + far_first(p, ROWS), ROWS) * CORES + c})
             return carry
         lax.fori_loop(1, ROWS, one, 0)
 
@@ -170,12 +173,12 @@
                 send_act(q, start, count)
 
     send(blk, mate, mate_sem, {"ctx": twin})
-    send(act.at[pl.ds(tokens - 16, 16)], halo, halo_sem, {"ctx": after})
     group = x * ROWS + y
     drain(mate, mate_sem.at[1])
     both[...] = blk[...] + mate[...]
     first_rates[c, few_of(group), :] = both[few_of(c), :]
     send_line(first_rates.at[c, few_of(group)], first_rates.at[c, few_of(group)], fy_sem)
+    send(act.at[pl.ds(tokens - 16, 16)], halo, halo_sem, {"ctx": after})
     send(both.at[slot_of(c)], pair_z, pair_sem, {"phase": above})
     send(act.at[pl.ds(tokens - 16, 16), far], halo_z.at[:, far], halo_z_sem,
          {"phase": above, "ctx": after})
@@ -384,9 +387,9 @@
     line_sum(0)
     line_sum(1)
     send_acts(3)
+    carries(0)
     drain(filt.at[0, pl.ds(0, (nx - 1) * ROWS * MODES)], px_sem.at[1])
     send(filt.at[c], filt.at[c], swap_sem, {"ctx": twin})
-    carries(0)
     carries(1)
     send_acts(4)
     drain(filt.at[0], swap_sem.at[1])

time: 59.2 us -> 58.3 us (0.985)
  Pallas kernels: 56.7 us -> 55.7 us
    pallas_call x1, Pallas kernels: 56.7 us -> 55.7 us  [local(): pl.pallas_call(functools.partial(kernel, phases, nx, tokens), out_shape=j...]
where the time goes in v4:
time: 58.3 us; the launch traced here: 58 us
  Pallas kernels  55.7 us (96%)
  local copies, waits for them, and re-layouts  2.29 us (4%)
    pallas_call x1, Pallas kernels, local(): pl.pallas_call(functools.partial(kernel, phases, nx, tokens), out_shape=j...  55.7 us
    unnamed x1, local copies, waits for them, and re-layouts  2.29 us

profile of v4, /device:TPU:1, one launch (start us, length us, event | category | flops | bytes accessed | tf_op | source)
XLA Modules:
  0.0 58.0 jit_solution(11848914444814124205)
XLA Ops:
  0.0 55.7 %shard_map.64 = bf16[128,4096]{1,0:T(8,128)(2,1)} custom-call(bf16[128,4096]{1,0:T(8,128)(2,1)} %bitcast.10, bf16[1,4096]{1,0:T(2,128)(2,1)} %gains.1, bf16[3,3,4096]{2,1,0:T(4,128)(2,1)} %bitcast.11, bf16[1,4096]{1,0:T(2,128)(2,1)} %skips.1, f32[16,64]{1,0:T(8,128)} %bitcast.12, f32[16,64]{1,0:T(8,128)} %bitcast.13), custom_call_target="tpu_custom_call" | custom-call | tf_op jit(solution)/shard_map/pallas_call | solution.py:446
  55.8 2.3 %copy.8 = bf16[1,128,4096]{2,1,0:T(8,128)(2,1)} copy(bf16[1,128,4096]{2,1,0:T(8,128)(2,1)} %bitcast.9) | data formatting | bytes 2097152

commit v5 on v4

--- a/solution.py
+++ b/solution.py
@@ -15,6 +15,7 @@
 PARTS = ((0,), (1, 2, 3))
 EARLY = 1
 PLAN = (((1, 0, 128),), ((2, 0, 128),), ((3, 0, 128),), (), ())
+CUTS = 2
 KINDS = 11
 F32 = jnp.float32
 BF16 = jnp.bfloat16
@@ -357,7 +358,6 @@
 
         state = tuple(
             cb[h, strided(h, k, r), :] for r in range(MODES))
-        lax.fori_loop(0, tokens // 4, one, state)
 
         def gather(i, carry):
             start = pl.multiple_of(i * 16, 16)
@@ -368,12 +368,17 @@
                     jnp.concatenate([low, high], axis=0).astype(BF16))
             return carry
 
-        lax.fori_loop(0, tokens // 16, gather, 0)
         part = pl.ds(q * wide, wide)
-        if q < near:
-            send(ob.at[:, part], out.at[:, part], z_sem, {"phase": above})
-        else:
-            pltpu.make_async_copy(ob.at[:, part], out.at[:, part], store_sem).start()
+        rows = tokens // CUTS
+        for cut in range(CUTS):
+            state = lax.fori_loop(cut * rows // 4, (cut + 1) * rows // 4, one, state)
+            lax.fori_loop(cut * rows // 16, (cut + 1) * rows // 16, gather, 0)
+            piece = pl.ds(cut * rows, rows)
+            if q < near:
+                send(ob.at[piece, part], out.at[piece, part], z_sem, {"phase": above})
+            else:
+                pltpu.make_async_copy(
+                    ob.at[piece, part], out.at[piece, part], store_sem).start()
 
     end_state(0)
     end_state(1)

time: 58.3 us -> 57.3 us (0.983)
  Pallas kernels: 55.7 us -> 54.8 us
    pallas_call x1, Pallas kernels: 55.7 us -> 54.8 us  [local(): pl.pallas_call(functools.partial(kernel, phases, nx, tokens), out_shape=j...]
where the time goes in v5:
time: 57.3 us; the launch traced here: 57.1 us
  Pallas kernels  54.8 us (96%)
  local copies, waits for them, and re-layouts  2.29 us (4%)
    pallas_call x1, Pallas kernels, local(): pl.pallas_call(functools.partial(kernel, phases, nx, tokens), out_shape=j...  54.8 us
    unnamed x1, local copies, waits for them, and re-layouts  2.29 us

profile of v5, /device:TPU:1, one launch (start us, length us, event | category | flops | bytes accessed | tf_op | source)
XLA Modules:
  0.0 57.1 jit_solution(16352437580456253922)
XLA Ops:
  0.0 54.8 %shard_map.64 = bf16[128,4096]{1,0:T(8,128)(2,1)} custom-call(bf16[128,4096]{1,0:T(8,128)(2,1)} %bitcast.10, bf16[1,4096]{1,0:T(2,128)(2,1)} %gains.1, bf16[3,3,4096]{2,1,0:T(4,128)(2,1)} %bitcast.11, bf16[1,4096]{1,0:T(2,128)(2,1)} %skips.1, f32[16,64]{1,0:T(8,128)} %bitcast.12, f32[16,64]{1,0:T(8,128)} %bitcast.13), custom_call_target="tpu_custom_call" | custom-call | tf_op jit(solution)/shard_map/pallas_call | solution.py:451
  54.8 2.3 %copy.8 = bf16[1,128,4096]{2,1,0:T(8,128)(2,1)} copy(bf16[1,128,4096]{2,1,0:T(8,128)(2,1)} %bitcast.9) | data formatting | bytes 2097152
